TPU v7x, 128 devices: a whole 4x4x4 slice. The times are simulated.
128 devices in a mesh: dp: 8 (over z, core), shard: 16 (over x, y).
Axes of the slice: x: 4, y: 4, z: 4, core: 2. Of those that a mesh axis runs over, the one named last changes fastest.
Arguments:
- tokens: bfloat16 [16, 2048, 1024], P('shard', 'dp'), may hold values from -6 to 6
- cotangent: bfloat16 [16, 2048, 1024], P('shard', 'dp'), may hold values from -6 to 6
- lengths: int32 [16, 4], P('shard'), may hold values from 1 to 1920, 2048 in all within a row
- weight_input: float32 [1024, 4096], P(('dp', 'shard')), may hold values from -0.1875 to 0.1875
- weight_output: float32 [2048, 1024], P(('dp', 'shard')), may hold values from -1 to 1
- weight_expand: float32 [1024, 6144], P(('dp', 'shard')), may hold values from -0.1875 to 0.1875
- weight_reduce: float32 [3072, 1024], P(('dp', 'shard')), may hold values from -0.109375 to 0.109375
- gains: float32 [2304], P(('dp', 'shard')), may hold values from 0.5 to 1.5
- first_input: float32 [1024, 4096], P(('dp', 'shard')), may hold values from -128 to 128
- first_output: float32 [2048, 1024], P(('dp', 'shard')), may hold values from -20 to 20
- first_expand: float32 [1024, 6144], P(('dp', 'shard')), may hold values from -64 to 64
- first_reduce: float32 [3072, 1024], P(('dp', 'shard')), may hold values from -64 to 64
- first_gains: float32 [2304], P(('dp', 'shard')), may hold values from -128 to 128
- second_input: float32 [1024, 4096], P(('dp', 'shard')), may hold values from 1723.5968 to 6881.28
- second_output: float32 [2048, 1024], P(('dp', 'shard')), may hold values from 49.152 to 196.608
- second_expand: float32 [1024, 6144], P(('dp', 'shard')), may hold values from 622.592 to 2490.368
- second_reduce: float32 [3072, 1024], P(('dp', 'shard')), may hold values from 622.592 to 2490.368
- second_gains: float32 [2304], P(('dp', 'shard')), may hold values from 1723.5968 to 6881.28
Outputs:
- block_out: bfloat16 [16, 2048, 1024], P('shard', 'dp')
- input_grad: float32 [16, 2048, 1024], P('shard', 'dp')
- new_input: float32 [1024, 4096], P(('dp', 'shard'))
- new_output: float32 [2048, 1024], P(('dp', 'shard'))
- new_expand: float32 [1024, 6144], P(('dp', 'shard'))
- new_reduce: float32 [3072, 1024], P(('dp', 'shard'))
- new_gains: float32 [2304], P(('dp', 'shard'))
- mean_input: float32 [1024, 4096], P(('dp', 'shard'))
- mean_output: float32 [2048, 1024], P(('dp', 'shard'))
- mean_expand: float32 [1024, 6144], P(('dp', 'shard'))
- mean_reduce: float32 [3072, 1024], P(('dp', 'shard'))
- mean_gains: float32 [2304], P(('dp', 'shard'))
- square_input: float32 [1024, 4096], P(('dp', 'shard'))
- square_output: float32 [2048, 1024], P(('dp', 'shard'))
- square_expand: float32 [1024, 6144], P(('dp', 'shard'))
- square_reduce: float32 [3072, 1024], P(('dp', 'shard'))
- square_gains: float32 [2304], P(('dp', 'shard'))
Inputs may be any that keep to these rules, and one draw needn't show every extreme that they name: `lengths`: each row sums to 2048; the longest sequence of every row has exactly 1920 tokens.
All inputs are finite; a program needn't handle non-finite values.
Results may differ from a plain program's by a relative error of at most 0.015.
Values may be sent and summed in bfloat16 or wider, within the bound.
A program may use at most 192 MiB of HBM per device.

v0:
```python
import jax
import jax.numpy as jnp
from jax import lax
from jax.sharding import PartitionSpec as P

D = 1024
H = 16
KV = 8
HD = 128
FF = 3072
STEP = 10


norm_eps = 1e-06
rope_base = 1000000.0
beta_one = 0.9
beta_two = 0.95
adam_eps = 1e-08
matrix_rate = 0.1
gain_rate = 0.5
matrix_decay = 0.1
masked_score = -1e30


def rms_scale(values, gain):
    return values * lax.rsqrt(jnp.mean(values * values, axis=-1, keepdims=True) + norm_eps) * gain


def rope_tables(positions, width):
    half = width // 2
    freq = rope_base ** (-(2.0 * jnp.arange(half, dtype=jnp.float32)) / width)
    angle = positions.astype(jnp.float32)[:, None] * freq[None, :]
    return (jnp.cos(angle), jnp.sin(angle))


def rotate(values, cosine, sine):
    half = values.shape[-1] // 2
    first = values[..., :half]
    second = values[..., half:]
    cos_b = cosine[:, None, :]
    sin_b = sine[:, None, :]
    return jnp.concatenate(
        [first * cos_b - second * sin_b, second * cos_b + first * sin_b], axis=-1
    )


def seq_layout(lengths, count):
    ends = jnp.cumsum(lengths)
    starts = ends - lengths
    index = jnp.arange(count, dtype=jnp.int32)
    segment = jnp.sum((index[:, None] >= ends[None, :]).astype(jnp.int32), axis=1)
    onehot = (segment[:, None] == jnp.arange(lengths.shape[0], dtype=jnp.int32)[None, :]).astype(
        jnp.int32
    )
    position = index - jnp.sum(onehot * starts[None, :], axis=1)
    return (segment, position)


def adam_step(weight, grad, first, second, rate, decay):
    first_new = beta_one * first + (1.0 - beta_one) * grad
    second_new = beta_two * second + (1.0 - beta_two) * grad * grad
    fix_one = 1.0 - beta_one**STEP
    fix_two = 1.0 - beta_two**STEP
    direction = first_new / fix_one / (jnp.sqrt(second_new / fix_two) + adam_eps)
    return (weight - rate * (direction + decay * weight), first_new, second_new)


def qk_prepare(query, key, gain_query, gain_key, cosine, sine):
    return (
        rotate(rms_scale(query, gain_query), cosine, sine),
        rotate(rms_scale(key, gain_key), cosine, sine),
    )


def swiglu(gate_up):
    return jax.nn.silu(gate_up[:, :FF]) * gate_up[:, FF:]


def to_heads(values, count):
    group = H // KV
    return values.reshape(count, KV, group, HD).transpose(1, 2, 0, 3).reshape(KV, group * count, HD)


def from_heads(values, count):
    group = H // KV
    return values.reshape(KV, group, count, HD).transpose(2, 0, 1, 3).reshape(count, H * HD)


def body(
    tokens,
    cotangent,
    lengths,
    weight_input,
    weight_output,
    weight_expand,
    weight_reduce,
    gains,
    first_input,
    first_output,
    first_expand,
    first_reduce,
    first_gains,
    second_input,
    second_output,
    second_expand,
    second_reduce,
    second_gains,
):
    count = tokens.shape[1]
    ranks = lax.axis_size("dp")
    rank = lax.axis_index("dp")
    whole = count * ranks
    group = H // KV
    scale = HD ** (-0.5)
    x_val = tokens[0].astype(jnp.float32)
    all_gains = lax.all_gather(gains, ("dp", "shard"), axis=0, tiled=True)
    gain_in = all_gains[:D]
    gain_mid = all_gains[D : 2 * D]
    gain_query = all_gains[2 * D : 2 * D + HD]
    gain_key = all_gains[2 * D + HD :]
    low_weights = (
        weight_input.astype(jnp.bfloat16),
        weight_output.astype(jnp.bfloat16),
        weight_expand.astype(jnp.bfloat16),
        weight_reduce.astype(jnp.bfloat16),
    )
    inner_rows = (
        lax.all_gather(low_weights[0], "shard", axis=0, tiled=True),
        lax.all_gather(low_weights[1], "shard", axis=0, tiled=True),
        lax.all_gather(low_weights[2], "shard", axis=0, tiled=True),
        lax.all_gather(low_weights[3], "shard", axis=0, tiled=True),
    )

    def forward_product(left, which):
        own_rows = inner_rows[which]
        return jnp.dot(
            left,
            lax.all_gather(own_rows, "dp", axis=0, tiled=True),
            preferred_element_type=jnp.float32,
        )

    def backward_product(grad, which):
        return lax.dot_general(
            grad,
            lax.all_gather(inner_rows[which], "dp", axis=0, tiled=True),
            (((1,), (1,)), ((), ())),
            preferred_element_type=jnp.float32,
        )

    def weight_grad(left, grad):
        return lax.psum_scatter(
            lax.dot_general(
                left, grad, (((0,), (0,)), ((), ())), preferred_element_type=jnp.float32
            ),
            ("dp", "shard"),
            scatter_dimension=0,
            tiled=True,
        )

    segment_all, position_all = seq_layout(lengths[0], whole)
    offset = rank * count
    segment_mine = lax.dynamic_slice_in_dim(segment_all, offset, count)
    position_mine = lax.dynamic_slice_in_dim(position_all, offset, count)
    row_segment = jnp.tile(segment_mine, group)
    row_index = jnp.tile(offset + jnp.arange(count, dtype=jnp.int32), group)
    key_index = jnp.arange(whole, dtype=jnp.int32)
    allowed = (row_segment[:, None] == segment_all[None, :]) & (
        key_index[None, :] <= row_index[:, None]
    )
    cosine, sine = rope_tables(position_mine, HD)
    normed_low = rms_scale(x_val, gain_in).astype(jnp.bfloat16)
    qkv = forward_product(normed_low, 0)
    query_raw = qkv[:, : H * HD].reshape(count, H, HD)
    key_raw = qkv[:, H * HD : (H + KV) * HD].reshape(count, KV, HD)
    value_low = qkv[:, (H + KV) * HD :].reshape(count, KV, HD).astype(jnp.bfloat16)
    query_rot, key_rot = qk_prepare(query_raw, key_raw, gain_query, gain_key, cosine, sine)
    query_heads = to_heads(query_rot.astype(jnp.bfloat16), count)
    key_heads = key_rot.astype(jnp.bfloat16).transpose(1, 0, 2)
    value_heads = value_low.transpose(1, 0, 2)
    keys_group, values_group = (
        lax.all_gather(key_heads, "dp", axis=1, tiled=True),
        lax.all_gather(value_heads, "dp", axis=1, tiled=True),
    )

    def head_forward(items):
        q_head, k_head, v_head = items
        scores = (
            lax.dot_general(
                q_head, k_head, (((1,), (1,)), ((), ())), preferred_element_type=jnp.float32
            )
            * scale
        )
        scores = jnp.where(allowed, scores, masked_score)
        top = jnp.max(scores, axis=-1, keepdims=True)
        expo = jnp.exp(scores - top)
        total = jnp.sum(expo, axis=-1, keepdims=True)
        probs = (expo / total).astype(jnp.bfloat16)
        mixed_head = jnp.dot(probs, v_head, preferred_element_type=jnp.float32)
        return (mixed_head, (top + jnp.log(total))[:, 0])

    mixed_heads, log_totals = lax.map(head_forward, (query_heads, keys_group, values_group))
    mixed_low = from_heads(mixed_heads, count).astype(jnp.bfloat16)
    hidden = x_val + forward_product(mixed_low, 1)
    normed_mid_low = rms_scale(hidden, gain_mid).astype(jnp.bfloat16)
    gate_up = forward_product(normed_mid_low, 2)
    act_low = swiglu(gate_up).astype(jnp.bfloat16)
    result = hidden + forward_product(act_low, 3)
    block_out = result.astype(jnp.bfloat16)[None]
    grad_low = cotangent[0]
    grad_val = grad_low.astype(jnp.float32)
    grad_reduce = weight_grad(act_low, grad_low)
    d_act = backward_product(grad_low, 3)
    unused, swiglu_pull = jax.vjp(swiglu, gate_up)
    d_gate_up = swiglu_pull(d_act)[0].astype(jnp.bfloat16)
    grad_expand = weight_grad(normed_mid_low, d_gate_up)
    d_normed_mid = backward_product(d_gate_up, 2)
    unused, mid_pull = jax.vjp(rms_scale, hidden, gain_mid)
    d_hidden_part, d_gain_mid = mid_pull(d_normed_mid)
    d_hidden = grad_val + d_hidden_part
    d_attended = d_hidden.astype(jnp.bfloat16)
    grad_output = weight_grad(mixed_low, d_attended)
    d_mixed = backward_product(d_attended, 1).astype(jnp.bfloat16)
    d_mixed_heads = to_heads(d_mixed, count)

    def head_backward(items):
        q_head, k_head, v_head, d_head, log_total = items
        scores = (
            lax.dot_general(
                q_head, k_head, (((1,), (1,)), ((), ())), preferred_element_type=jnp.float32
            )
            * scale
        )
        probs = jnp.exp(jnp.where(allowed, scores - log_total[:, None], masked_score))
        d_probs = lax.dot_general(
            d_head, v_head, (((1,), (1,)), ((), ())), preferred_element_type=jnp.float32
        )
        inner = jnp.sum(probs * d_probs, axis=-1, keepdims=True)
        d_scores = (probs * (d_probs - inner)).astype(jnp.bfloat16)
        d_query = jnp.dot(d_scores, k_head, preferred_element_type=jnp.float32) * scale
        d_key = (
            lax.dot_general(
                d_scores, q_head, (((0,), (0,)), ((), ())), preferred_element_type=jnp.float32
            )
            * scale
        )
        d_value = lax.dot_general(
            probs.astype(jnp.bfloat16),
            d_head,
            (((0,), (0,)), ((), ())),
            preferred_element_type=jnp.float32,
        )
        return (d_query, d_key, d_value)

    d_query_heads, d_key_group, d_value_group = lax.map(
        head_backward, (query_heads, keys_group, values_group, d_mixed_heads, log_totals)
    )
    d_key_mine, d_value_mine = (
        lax.psum_scatter(
            d_key_group.astype(jnp.bfloat16), "dp", scatter_dimension=1, tiled=True
        ).astype(jnp.float32),
        lax.psum_scatter(
            d_value_group.astype(jnp.bfloat16), "dp", scatter_dimension=1, tiled=True
        ).astype(jnp.float32),
    )
    d_query = from_heads(d_query_heads, count).reshape(count, H, HD)
    d_key = d_key_mine.transpose(1, 0, 2)
    d_value = d_value_mine.transpose(1, 0, 2)

    def qk_only(query, key, gain_q, gain_k):
        return qk_prepare(query, key, gain_q, gain_k, cosine, sine)

    unused, qk_pull = jax.vjp(qk_only, query_raw, key_raw, gain_query, gain_key)
    d_query_raw, d_key_raw, d_gain_query, d_gain_key = qk_pull((d_query, d_key))
    d_qkv = jnp.concatenate(
        [
            d_query_raw.reshape(count, H * HD),
            d_key_raw.reshape(count, KV * HD),
            d_value.reshape(count, KV * HD),
        ],
        axis=1,
    ).astype(jnp.bfloat16)
    grad_input = weight_grad(normed_low, d_qkv)
    d_normed = backward_product(d_qkv, 0)
    unused, in_pull = jax.vjp(rms_scale, x_val, gain_in)
    d_x_part, d_gain_in = in_pull(d_normed)
    input_grad = (d_hidden + d_x_part)[None]
    gain_terms = jnp.concatenate([d_gain_in, d_gain_mid, d_gain_query, d_gain_key])
    grad_gains = lax.psum_scatter(gain_terms, ("dp", "shard"), scatter_dimension=0, tiled=True)
    new_input, mean_input, square_input = adam_step(
        weight_input, grad_input, first_input, second_input, matrix_rate, matrix_decay
    )
    new_output, mean_output, square_output = adam_step(
        weight_output, grad_output, first_output, second_output, matrix_rate, matrix_decay
    )
    new_expand, mean_expand, square_expand = adam_step(
        weight_expand, grad_expand, first_expand, second_expand, matrix_rate, matrix_decay
    )
    new_reduce, mean_reduce, square_reduce = adam_step(
        weight_reduce, grad_reduce, first_reduce, second_reduce, matrix_rate, matrix_decay
    )
    new_gains, mean_gains, square_gains = adam_step(
        gains, grad_gains, first_gains, second_gains, gain_rate, 0.0
    )
    return (
        block_out,
        input_grad,
        new_input,
        new_output,
        new_expand,
        new_reduce,
        new_gains,
        mean_input,
        mean_output,
        mean_expand,
        mean_reduce,
        mean_gains,
        square_input,
        square_output,
        square_expand,
        square_reduce,
        square_gains,
    )


def solution(mesh):
    placed = (
        P("shard", "dp", None),
        P("shard", "dp", None),
        P("shard", None),
        P(("dp", "shard"), None),
        P(("dp", "shard"), None),
        P(("dp", "shard"), None),
        P(("dp", "shard"), None),
        P(("dp", "shard")),
        P(("dp", "shard"), None),
        P(("dp", "shard"), None),
        P(("dp", "shard"), None),
        P(("dp", "shard"), None),
        P(("dp", "shard")),
        P(("dp", "shard"), None),
        P(("dp", "shard"), None),
        P(("dp", "shard"), None),
        P(("dp", "shard"), None),
        P(("dp", "shard")),
    )
    return jax.shard_map(
        body,
        mesh=mesh,
        in_specs=placed,
        out_specs=(
            P("shard", "dp", None),
            P("shard", "dp", None),
            P(("dp", "shard"), None),
            P(("dp", "shard"), None),
            P(("dp", "shard"), None),
            P(("dp", "shard"), None),
            P(("dp", "shard")),
            P(("dp", "shard"), None),
            P(("dp", "shard"), None),
            P(("dp", "shard"), None),
            P(("dp", "shard"), None),
            P(("dp", "shard")),
            P(("dp", "shard"), None),
            P(("dp", "shard"), None),
            P(("dp", "shard"), None),
            P(("dp", "shard"), None),
            P(("dp", "shard")),
        ),
        check_vma=False,
    )
```

profile of v0, /device:TPU:0, one launch (start us, length us, event | category | flops | bytes accessed | tf_op | source)
XLA Modules:
  0.0 2436.8 jit_solution(14375930849867241453)
XLA Ops:
  8.9 47.0 %all-gather.9.cloned.1.call-done = bf16[128,4096]{1,0:T(8,128)(2,1)} async-done(((bf16[8,4096]{1,0:T(8,128)(2,1)}), bf16[128,4096]{1,0:T(8,128)(2,1)}) %all-gather.9.cloned.1.call-update) | async-done | bytes 1048592 | tf_op jit(solution)/shard_map/all_gather | solution.py:128
  61.4 65.4 %all-reduce.6 = f32[2304]{0:T(1024)S(1)} all-reduce(f32[2304]{0:T(1024)S(1)} %dynamic-update-slice), channel_id=1, replica_groups=mesh['dp'=8,'shard'=16] {'dp','shard'}, use_global_device_ids=true, to_apply=%add.6 | all-reduce | flops 2304 | bytes 18432
  127.3 6.0 fusion.74
  140.6 23.6 all_gather.42
  165.1 25.6 %all_gather.46 = bf16[384,1024]{1,0:T(8,128)(2,1)} all-gather(bf16[24,1024]{1,0:T(8,128)(2,1)S(1)} %convert_element_type.101), channel_id=1, replica_groups=mesh['dp'=8,'shard'=16] {'shard'}, dimensions={0}, use_global_device_ids=true | all-gather | bytes 835584 | tf_op jit(solution)/shard_map/all_gather | solution.py:131
  201.2 6.6 copy.166
  207.8 19.7 all-gather.15.cloned.1.call-done
  227.6 51.6 %while.30 = (s32[]{:T(128)}, bf16[8,512,128]{2,1,0:T(8,128)(2,1)S(1)}, f32[8,512]{1,0:T(8,128)}, bf16[8,512,128]{2,1,0:T(8,128)(2,1)S(1)}, bf16[8,2048,128]{2,1,...) while((s32[]{:T(128)}, ...), condition=%wide.region_9.10_spmd.clone.clone, body=%wide.region_6.9_spmd.clone.sunk.clone | while | flops 548404736 | bytes 14059625 | solution.py:201
  227.6 2.5 fusion.147
  234.0 2.4 fusion.147
  240.5 2.4 fusion.147
  246.9 2.4 fusion.147
  253.4 2.4 fusion.147
  259.8 2.4 fusion.147
  266.2 2.4 fusion.147
  272.7 2.5 fusion.147
  280.7 3.9 multiply_reduce_fusion.8
  284.7 45.7 %all-gather.21.cloned.1.call-done = bf16[1024,6144]{1,0:T(8,128)(2,1)} async-done(((bf16[128,6144]{1,0:T(8,128)(2,1)}), bf16[1024,6144]{1,0:T(8,128)(2,1)}) %all-gather.21.cloned.1.call-update) | async-done | bytes 12582928 | tf_op jit(solution)/shard_map/all_gather | solution.py:138
  330.4 10.1 fusion.90
  340.5 33.0 %all-gather.23.cloned.1.call-done = bf16[3072,1024]{1,0:T(8,128)(2,1)} async-done(((bf16[384,1024]{1,0:T(8,128)(2,1)}), bf16[3072,1024]{1,0:T(8,128)(2,1)}) %all-gather.23.cloned.1.call-update) | async-done | bytes 6291472 | tf_op jit(solution)/shard_map/all_gather | solution.py:138
  373.5 22.8 fusion.68
  396.3 11.0 multiply_reduce_fusion.5
  408.8 3.9 convolution_convert_fusion
  415.7 133.8 %while.31 = (s32[]{:T(128)}, f32[8,512,128]{2,1,0:T(8,128)}, bf16[8,2048,128]{1,2,0:T(8,128)(2,1)}, bf16[8,2048,128]{1,2,0:T(8,128)(2,1)}, bf16[8,512,128]{2,1,0...) while((s32[]{:T(128)}, f32[8,512,128]{2,1,0:T(8,128)}, ...), condition=%wide.region_14.15_spmd.clone.clone, body=%wide.region_12.14_spmd.clone.sunk.clone | while | flops 1355349504 | bytes 62679260 | solution.py:254
  415.7 2.1 fusion.158
  418.6 3.0 multiply_reduce_fusion.12
  423.7 2.5 fusion.159
  428.9 3.6 fusion.161
  435.3 3.0 multiply_reduce_fusion.12
  440.4 2.5 fusion.159
  445.6 3.6 fusion.161
  452.0 3.0 multiply_reduce_fusion.12
  457.1 2.5 fusion.159
  462.3 3.6 fusion.161
  468.7 3.0 multiply_reduce_fusion.12
  473.8 2.5 fusion.159
  479.0 3.6 fusion.161
  485.4 3.0 multiply_reduce_fusion.12
  490.5 2.5 fusion.159
  495.7 3.6 fusion.161
  502.1 3.0 multiply_reduce_fusion.12
  507.2 2.5 fusion.159
  512.4 3.6 fusion.161
  518.9 3.0 multiply_reduce_fusion.12
  523.9 2.5 fusion.159
  529.1 3.6 fusion.161
  532.7 2.1 fusion.158
  535.6 3.0 multiply_reduce_fusion.12
  540.6 2.5 fusion.159
  545.9 3.6 fusion.161
  550.7 4.5 fusion.69
  556.8 6.4 fusion.62
  563.2 13.6 fusion.66
  581.8 2.9 multiply_reduce_fusion.1
  584.9 4.0 fusion.46
  592.3 34.7 %reduce-scatter.7.cloned.1.call-done = bf16[8,256,128]{1,2,0:T(8,128)(2,1)} async-done(((bf16[8,2048,128]{1,2,0:T(8,128)(2,1)}), bf16[8,256,128]{1,2,0:T(8,128)(2,1)}) %reduce-scatter.7.cloned.1.call-update) | async-done | bytes 524304 | tf_op jit(solution)/shard_map/reduce_scatter | solution.py:258
  631.6 9.8 fusion.59
  641.4 6.0 fusion.50
  647.4 6.6 fusion.52
  654.1 66.7 %all-reduce.7 = f32[2304]{0:T(1024)S(1)} all-reduce(f32[2304]{0:T(1024)S(1)} %pad_maximum_fusion.4), channel_id=8, replica_groups=mesh['dp'=8,'shard'=16] {'dp','shard'}, use_global_device_ids=true, to_apply=%region_28.29.clone | all-reduce | flops 2304 | bytes 18432
  724.1 557.7 %reduce-scatter.13.cloned.1.call-done = f32[16,1024]{1,0:T(8,128)} async-done(((f32[2048,1024]{1,0:T(8,128)}), f32[16,1024]{1,0:T(8,128)}) %reduce-scatter.13.cloned.1.call-update) | async-done | bytes 65552 | tf_op jit(solution)/shard_map/reduce_scatter | solution.py:151
  1283.4 220.1 %reduce-scatter.17.cloned.1.call-done = f32[24,1024]{1,0:T(8,128)} async-done(((f32[3072,1024]{1,0:T(8,128)}), f32[24,1024]{1,0:T(8,128)}) %reduce-scatter.17.cloned.1.call-update) | async-done | bytes 98320 | tf_op jit(solution)/shard_map/reduce_scatter | solution.py:151
  1505.3 248.8 %reduce-scatter.15.cloned.1.call-done = f32[8,6144]{1,0:T(8,128)} async-done(((f32[1024,6144]{1,0:T(8,128)}), f32[8,6144]{1,0:T(8,128)}) %reduce-scatter.15.cloned.1.call-update) | async-done | bytes 196624 | tf_op jit(solution)/shard_map/reduce_scatter | solution.py:151
  1755.9 672.2 %reduce-scatter.11.cloned.1.call-done = f32[8,4096]{1,0:T(8,128)} async-done(((f32[1024,4096]{1,0:T(8,128)}), f32[8,4096]{1,0:T(8,128)}) %reduce-scatter.11.cloned.1.call-update) | async-done | bytes 131088 | tf_op jit(solution)/shard_map/reduce_scatter | solution.py:151
  (355 shorter events, 146.6 us)
Async XLA Ops:
  7.2 48.6 %all-gather.9.cloned.1.call-start = ((), (), s32[]{:S(2)}) async-start(), calls=%async_computation.6 | async-start | bytes 1114112 | tf_op jit(solution)/shard_map/all_gather | solution.py:128
  8.8 118.5 %all-gather.11.cloned.1.call-start = ((), (), s32[]{:S(2)}) async-start(), calls=%async_computation.7 | async-start | bytes 9437184 | tf_op jit(solution)/shard_map/all_gather | solution.py:138
  55.8 108.5 %all-gather.19.cloned.1.call-start = ((), (), s32[]{:S(2)}) async-start(), calls=%async_computation.11 | async-start | bytes 1671168 | tf_op jit(solution)/shard_map/all_gather | solution.py:130
  57.5 143.7 %all-gather.13.cloned.1.call-start = ((), (), s32[]{:S(2)}) async-start(), calls=%async_computation.8 | async-start | bytes 4718592 | tf_op jit(solution)/shard_map/all_gather | solution.py:181
  58.8 74.5 %copy-start.52 = (f32[256]{0:T(256)}, f32[256]{0:T(256)S(1)}, u32[]{:S(2)}) copy-start(f32[256]{0:T(256)S(1)} %fusion.57) | copy-start | bytes 3076
  126.8 6.5 copy-start.50
  126.9 9.9 copy-start.56
  126.9 71.2 %copy-start.54 = (f32[128]{0:T(128)}, f32[128]{0:T(128)S(1)}, u32[]{:S(2)}) copy-start(f32[128]{0:T(128)S(1)} %get-tuple-element.396) | copy-start | bytes 1540
  126.9 6.4 copy-start.37
  127.2 63.7 %copy-start.33 = (f32[256,64]{0,1:T(8,128)}, f32[256,64]{0,1:T(8,128)S(1)}, u32[]{:S(2)}) copy-start(f32[256,64]{0,1:T(8,128)S(1)} %get-tuple-element.398) | copy-start | bytes 196612
  127.2 63.8 %copy-start.31 = (f32[256,64]{0,1:T(8,128)}, f32[256,64]{0,1:T(8,128)S(1)}, u32[]{:S(2)}) copy-start(f32[256,64]{0,1:T(8,128)S(1)} %get-tuple-element.397) | copy-start | bytes 196612
  136.7 3.8 copy-start.41
  137.5 27.6 %copy-start.39 = (f32[24,1024]{1,0:T(8,128)S(1)}, f32[24,1024]{1,0:T(8,128)}, u32[]{:S(2)}) copy-start(f32[24,1024]{1,0:T(8,128)} %param.28) | copy-start | bytes 294916
  138.4 89.2 %all-gather.15.cloned.1.call-start = ((), (), s32[]{:S(2)}) async-start(), calls=%async_computation.9 | async-start | bytes 4718592 | tf_op jit(solution)/shard_map/all_gather | solution.py:182
  140.5 140.2 %all-gather.17.cloned.1.call-start = ((), (), s32[]{:S(2)}) async-start(), calls=%async_computation.10 | async-start | bytes 4718592 | tf_op jit(solution)/shard_map/all_gather | solution.py:138
  164.3 166.1 %all-gather.21.cloned.1.call-start = ((), (), s32[]{:S(2)}) async-start(), calls=%async_computation.12 | async-start | bytes 14155776 | tf_op jit(solution)/shard_map/all_gather | solution.py:138
  165.0 208.4 %all-gather.23.cloned.1.call-start = ((), (), s32[]{:S(2)}) async-start(), calls=%async_computation.13 | async-start | bytes 7077888 | tf_op jit(solution)/shard_map/all_gather | solution.py:138
  190.7 399.5 %reduce-scatter.9.cloned.1.call-start = ((), (), s32[]{:S(2)}) async-start(), calls=%async_computation.15 | async-start | bytes 4718592 | tf_op jit(solution)/shard_map/reduce_scatter | solution.py:261
  191.1 8.1 copy-start.26
  191.2 8.0 copy-start.28
  194.6 4.6 copy-start.1
  201.2 26.4 %copy-start.59 = (s32[1,2,2,128]{3,1,2,0:T(2,128)S(1)}, s32[1,2,2,128]{3,1,2,0:T(2,128)}, u32[]{:S(2)}) copy-start(s32[1,2,2,128]{3,1,2,0:T(2,128)} %copy.204) | copy-start | bytes 6148
  201.2 26.4 %copy-start.60 = (s32[1,2,2,128]{3,1,2,0:T(2,128)S(1)}, s32[1,2,2,128]{3,1,2,0:T(2,128)}, u32[]{:S(2)}) copy-start(s32[1,2,2,128]{3,1,2,0:T(2,128)} %copy.205) | copy-start | bytes 6148
  227.6 53.2 %copy-start.13 = (bf16[1,256,1024]{2,1,0:T(8,128)(2,1)S(1)}, bf16[1,256,1024]{2,1,0:T(8,128)(2,1)}, u32[]{:S(2)}) copy-start(bf16[1,256,1024]{2,1,0:T(8,128)(2,1)} %param.22) | copy-start | bytes 1572868
  280.7 3.9 copy-start.9
  330.4 43.1 %copy-start.23 = (bf16[1,256,1024]{2,1,0:T(8,128)(2,1)S(1)}, bf16[1,256,1024]{2,1,0:T(8,128)(2,1)}, u32[]{:S(2)}) copy-start(bf16[1,256,1024]{2,1,0:T(8,128)(2,1)} %param.23) | copy-start | bytes 1572868
  408.8 141.4 %copy-start.7 = (f32[256,1024]{1,0:T(8,128)}, f32[256,1024]{1,0:T(8,128)S(1)}, u32[]{:S(2)}) copy-start(f32[256,1024]{1,0:T(8,128)S(1)} %fusion.53) | copy-start | bytes 3145732
  415.7 5.9 copy-start.11
  432.5 5.9 copy-start.11
  449.2 5.9 copy-start.11
  465.9 5.9 copy-start.11
  482.6 5.9 copy-start.11
  495.7 3.6 copy-start.12
  499.3 5.9 copy-start.11
  512.4 3.6 copy-start.12
  516.0 5.9 copy-start.11
  532.7 5.9 copy-start.11
  549.5 77.5 %reduce-scatter.7.cloned.1.call-start = ((), (), s32[]{:S(2)}) async-start(), calls=%async_computation.14 | async-start | bytes 4718592 | tf_op jit(solution)/shard_map/reduce_scatter | solution.py:258
  550.1 731.7 %reduce-scatter.13.cloned.1.call-start = ((), (), s32[]{:S(2)}) async-start(), calls=%async_computation.17 | async-start | bytes 8454144 | tf_op jit(solution)/shard_map/reduce_scatter | solution.py:151
  555.2 948.3 %reduce-scatter.17.cloned.1.call-start = ((), (), s32[]{:S(2)}) async-start(), calls=%async_computation.19 | async-start | bytes 12681216 | tf_op jit(solution)/shard_map/reduce_scatter | solution.py:151
  563.2 1190.9 %reduce-scatter.15.cloned.1.call-start = ((), (), s32[]{:S(2)}) async-start(), calls=%async_computation.18 | async-start | bytes 25362432 | tf_op jit(solution)/shard_map/reduce_scatter | solution.py:151
  576.9 1851.2 %reduce-scatter.11.cloned.1.call-start = ((), (), s32[]{:S(2)}) async-start(), calls=%async_computation.16 | async-start | bytes 16908288 | tf_op jit(solution)/shard_map/reduce_scatter | solution.py:151
  580.9 3.8 copy-start.3
  580.9 3.8 copy-start.4
  588.9 39.2 %copy-start.32 = (f32[256,64]{0,1:T(8,128)S(1)}, f32[256,64]{0,1:T(8,128)}, u32[]{:S(2)}) copy-start(f32[256,64]{0,1:T(8,128)} %copy-done.31) | copy-start | bytes 196612
  588.9 39.2 %copy-start.34 = (f32[256,64]{0,1:T(8,128)S(1)}, f32[256,64]{0,1:T(8,128)}, u32[]{:S(2)}) copy-start(f32[256,64]{0,1:T(8,128)} %copy-done.33) | copy-start | bytes 196612
  588.9 39.4 %copy-start.6 = (f32[256,8,128]{0,2,1:T(8,128)S(1)}, f32[256,8,128]{0,2,1:T(8,128)}, u32[]{:S(2)}) copy-start(f32[256,8,128]{0,2,1:T(8,128)} %copy-done.5) | copy-start | bytes 3145732
  588.9 39.4 %copy-start.47 = (f32[256,8]{0,1:T(8,128)S(1)}, f32[256,8]{0,1:T(8,128)}, u32[]{:S(2)}) copy-start(f32[256,8]{0,1:T(8,128)} %copy-done.46) | copy-start | bytes 24580
  589.0 39.4 %copy-start.57 = (f32[128]{0:T(128)S(1)}, f32[128]{0:T(128)}, u32[]{:S(2)}) copy-start(f32[128]{0:T(128)} %copy-done.56) | copy-start | bytes 1540
  592.3 36.9 %copy-start.49 = (f32[256,8]{0,1:T(8,128)S(1)}, f32[256,8]{0,1:T(8,128)}, u32[]{:S(2)}) copy-start(f32[256,8]{0,1:T(8,128)} %copy-done.48) | copy-start | bytes 24580
  631.5 9.8 copy-start.20
  641.4 6.0 copy-start.15
  641.4 6.0 copy-start.19
  641.4 6.0 copy-start.21
  647.4 6.7 copy-start.58
  647.4 6.7 copy-start.61
  647.4 73.4 %copy-start.53 = (f32[256]{0:T(256)S(1)}, f32[256]{0:T(256)}, u32[]{:S(2)}) copy-start(f32[256]{0:T(256)} %copy-done.52) | copy-start | bytes 3076
  647.4 75.4 %copy-start.8 = (f32[256,1024]{1,0:T(8,128)S(1)}, f32[256,1024]{1,0:T(8,128)}, u32[]{:S(2)}) copy-start(f32[256,1024]{1,0:T(8,128)} %copy-done.7) | copy-start | bytes 3145732
  654.1 627.8 %copy-start.42 = (f32[16,1024]{1,0:T(8,128)S(1)}, f32[16,1024]{1,0:T(8,128)}, u32[]{:S(2)}) copy-start(f32[16,1024]{1,0:T(8,128)} %param.26) | copy-start | bytes 196612
  654.1 849.4 %copy-start.40 = (f32[24,1024]{1,0:T(8,128)S(1)}, f32[24,1024]{1,0:T(8,128)}, u32[]{:S(2)}) copy-start(f32[24,1024]{1,0:T(8,128)} %param.28) | copy-start | bytes 294916
  654.1 1100.0 %copy-start.35 = (f32[8,6144]{1,0:T(8,128)S(1)}, f32[8,6144]{1,0:T(8,128)}, u32[]{:S(2)}) copy-start(f32[8,6144]{1,0:T(8,128)} %param.27) | copy-start | bytes 589828
  654.1 1100.0 %copy-start.43 = (f32[8,6144]{1,0:T(8,128)S(1)}, f32[8,6144]{1,0:T(8,128)}, u32[]{:S(2)}) copy-start(f32[8,6144]{1,0:T(8,128)} %param.32) | copy-start | bytes 589828
  654.1 1100.0 %copy-start.44 = (f32[8,6144]{1,0:T(8,128)S(1)}, f32[8,6144]{1,0:T(8,128)}, u32[]{:S(2)}) copy-start(f32[8,6144]{1,0:T(8,128)} %param.37) | copy-start | bytes 589828
  654.1 1774.0 %copy-start.36 = (f32[8,4096]{1,0:T(8,128)S(1)}, f32[8,4096]{1,0:T(8,128)}, u32[]{:S(2)}) copy-start(f32[8,4096]{1,0:T(8,128)} %param.25) | copy-start | bytes 393220
  (33 other events, 75.9 us)
Sparse Core Ops, SparseCore 0:
  10.7 45.0 all-gather.8
  57.5 50.3 all-gather.10
  110.7 43.4 all-gather.18
  156.3 35.8 all-gather.12
  194.4 33.1 all-gather.14
  229.1 32.1 all-gather.16
  263.0 67.3 all-gather.20
  332.1 41.3 all-gather.22
  549.6 38.1 reduce-scatter.8
  590.0 36.9 reduce-scatter.6
  629.4 652.4 reduce-scatter.12
  1287.5 216.0 reduce-scatter.16
  1509.7 244.2 reduce-scatter.14
  1756.4 671.6 reduce-scatter.10
where the time goes:
time: 2450 us; the launch traced here: 2440 us
  waiting for transfers between devices  1880 us (77%)
  matrix products  242 us (10%)
  blocking collectives  181 us (7%)
  local copies, waits for them, and re-layouts  72.1 us (3%)
  other arithmetic  44.3 us (2%)
    reduce_scatter x4, waiting for transfers between devices, weight_grad(): lax.psum_scatter(lax.dot_general(left, grad, (((0,), (0,)), ((), ())), pr...  1700 us
    unnamed x2, blocking collectives  132 us
    all_gather x4, waiting for transfers between devices, forward_product(): lax.all_gather(own_rows, 'dp', axis=0, tiled=True)  78.7 us
  transfers between devices with their start and end apart: 14, of which 9 were waited for; matrix products, arithmetic and copies ran while one was open for 7% of the time, Pallas kernels for 0%

commit v1 on v0

v1 whole, which is shorter than its diff:
```python
import jax
import jax.numpy as jnp
from jax import lax
from jax.sharding import PartitionSpec as P

D = 1024
H = 16
KV = 8
HD = 128
FF = 3072
STEP = 10


norm_eps = 1e-06
rope_base = 1000000.0
beta_one = 0.9
beta_two = 0.95
adam_eps = 1e-08
matrix_rate = 0.1
gain_rate = 0.5
matrix_decay = 0.1
masked_score = -1e30


def rms_scale(values, gain):
    return values * lax.rsqrt(jnp.mean(values * values, axis=-1, keepdims=True) + norm_eps) * gain


def rope_tables(positions, width):
    half = width // 2
    freq = rope_base ** (-(2.0 * jnp.arange(half, dtype=jnp.float32)) / width)
    angle = positions.astype(jnp.float32)[:, None] * freq[None, :]
    return (jnp.cos(angle), jnp.sin(angle))


def rotate(values, cosine, sine):
    half = values.shape[-1] // 2
    first = values[..., :half]
    second = values[..., half:]
    cos_b = cosine[:, None, :]
    sin_b = sine[:, None, :]
    return jnp.concatenate(
        [first * cos_b - second * sin_b, second * cos_b + first * sin_b], axis=-1
    )


def seq_layout(lengths, count):
    ends = jnp.cumsum(lengths)
    starts = ends - lengths
    index = jnp.arange(count, dtype=jnp.int32)
    segment = jnp.sum((index[:, None] >= ends[None, :]).astype(jnp.int32), axis=1)
    onehot = (segment[:, None] == jnp.arange(lengths.shape[0], dtype=jnp.int32)[None, :]).astype(
        jnp.int32
    )
    position = index - jnp.sum(onehot * starts[None, :], axis=1)
    return (segment, position)


def adam_step(weight, grad, first, second, rate, decay):
    first_new = beta_one * first + (1.0 - beta_one) * grad
    second_new = beta_two * second + (1.0 - beta_two) * grad * grad
    fix_one = 1.0 - beta_one**STEP
    fix_two = 1.0 - beta_two**STEP
    direction = first_new / fix_one / (jnp.sqrt(second_new / fix_two) + adam_eps)
    return (weight - rate * (direction + decay * weight), first_new, second_new)


def qk_prepare(query, key, gain_query, gain_key, cosine, sine):
    return (
        rotate(rms_scale(query, gain_query), cosine, sine),
        rotate(rms_scale(key, gain_key), cosine, sine),
    )


def swiglu(gate_up):
    return jax.nn.silu(gate_up[:, :FF]) * gate_up[:, FF:]


def split_columns(rows, widths):
    parts = []
    start = 0
    ranks = lax.axis_size("dp")
    for width in widths:
        part = rows[:, start : start + width]
        parts.append(part.reshape(rows.shape[0], ranks, width // ranks))
        start += width
    return jnp.concatenate(parts, axis=2).transpose(1, 0, 2)


def join_columns(blocks, widths):
    ranks = blocks.shape[0]
    parts = []
    start = 0
    for width in widths:
        part = blocks[:, :, start : start + width // ranks]
        parts.append(part.transpose(1, 0, 2).reshape(blocks.shape[1], width))
        start += width // ranks
    return jnp.concatenate(parts, axis=1)


IN_WIDTHS = (H * HD, KV * HD, KV * HD)
EXPAND_WIDTHS = (FF, FF)


def gather_columns(weight, widths):
    blocks = split_columns(weight.astype(jnp.bfloat16), widths)
    mine = lax.all_to_all(blocks, "dp", 0, 0)
    whole = lax.all_gather(mine, "shard", axis=1, tiled=True)
    return whole.reshape(-1, whole.shape[-1])


def gather_rows(weight):
    return lax.all_gather(weight.astype(jnp.bfloat16), "shard", axis=0, tiled=True)


def scatter_columns(grad, widths):
    ranks = lax.axis_size("dp")
    low = grad.astype(jnp.bfloat16).reshape(ranks, grad.shape[0] // ranks, grad.shape[1])
    mine = lax.psum_scatter(low, "shard", scatter_dimension=1, tiled=True)
    return join_columns(lax.all_to_all(mine, "dp", 0, 0).astype(jnp.float32), widths)


def scatter_rows(grad):
    return lax.psum_scatter(
        grad.astype(jnp.bfloat16), "shard", scatter_dimension=0, tiled=True
    ).astype(jnp.float32)


def gather_tokens(block):
    return lax.all_gather(block, "dp", axis=0, tiled=True)


def scatter_tokens(partial):
    return lax.psum_scatter(
        partial.astype(jnp.bfloat16), "dp", scatter_dimension=0, tiled=True
    ).astype(jnp.float32)


def dot(a, b):
    return jnp.dot(a, b, preferred_element_type=jnp.float32)


def dot_t(a, b):
    return lax.dot_general(a, b, (((1,), (1,)), ((), ())), preferred_element_type=jnp.float32)


def t_dot(a, b):
    return lax.dot_general(a, b, (((0,), (0,)), ((), ())), preferred_element_type=jnp.float32)


def body(
    tokens,
    cotangent,
    lengths,
    weight_input,
    weight_output,
    weight_expand,
    weight_reduce,
    gains,
    first_input,
    first_output,
    first_expand,
    first_reduce,
    first_gains,
    second_input,
    second_output,
    second_expand,
    second_reduce,
    second_gains,
):
    ranks = lax.axis_size("dp")
    count = tokens.shape[1]
    whole = count * ranks
    group = H // KV
    scale = HD ** (-0.5)
    half = FF // ranks
    x_val = tokens[0].astype(jnp.float32)
    all_gains = lax.all_gather(
        lax.all_gather(gains, "shard", axis=0, tiled=True), "dp", axis=0, tiled=True
    )
    gain_in = all_gains[:D]
    gain_mid = all_gains[D : 2 * D]
    gain_query = all_gains[2 * D : 2 * D + HD]
    gain_key = all_gains[2 * D + HD :]
    w_in = gather_columns(weight_input, IN_WIDTHS)
    w_out = gather_rows(weight_output)
    w_exp = gather_columns(weight_expand, EXPAND_WIDTHS)
    w_red = gather_rows(weight_reduce)

    segment, position = seq_layout(lengths[0], whole)
    index = jnp.arange(whole, dtype=jnp.int32)
    allowed = (segment[:, None] == segment[None, :]) & (index[None, :] <= index[:, None])
    cosine, sine = rope_tables(position, HD)

    normed = gather_tokens(rms_scale(x_val, gain_in).astype(jnp.bfloat16))
    qkv = dot(normed, w_in)
    query_raw = qkv[:, : group * HD].reshape(whole, group, HD)
    key_raw = qkv[:, group * HD : (group + 1) * HD].reshape(whole, 1, HD)
    value = qkv[:, (group + 1) * HD :].astype(jnp.bfloat16)
    query_rot, key_rot = qk_prepare(query_raw, key_raw, gain_query, gain_key, cosine, sine)
    query = query_rot.astype(jnp.bfloat16)
    key = key_rot.astype(jnp.bfloat16)[:, 0]

    def head_forward(q_head):
        scores = jnp.where(allowed, dot_t(q_head, key) * scale, masked_score)
        top = jnp.max(scores, axis=-1, keepdims=True)
        expo = jnp.exp(scores - top)
        total = jnp.sum(expo, axis=-1, keepdims=True)
        probs = (expo / total).astype(jnp.bfloat16)
        return (dot(probs, value), (top + jnp.log(total))[:, 0])

    mixed, log_totals = lax.map(head_forward, query.transpose(1, 0, 2))
    mixed_low = mixed.transpose(1, 0, 2).reshape(whole, group * HD).astype(jnp.bfloat16)
    hidden = x_val + scatter_tokens(dot(mixed_low, w_out))
    normed_mid = gather_tokens(rms_scale(hidden, gain_mid).astype(jnp.bfloat16))
    gate_up = dot(normed_mid, w_exp)

    def act_of(gu):
        return jax.nn.silu(gu[:, :half]) * gu[:, half:]

    act, act_pull = jax.vjp(act_of, gate_up)
    act_low = act.astype(jnp.bfloat16)
    block_out = (hidden + scatter_tokens(dot(act_low, w_red))).astype(jnp.bfloat16)[None]

    grad_val = cotangent[0].astype(jnp.float32)
    grad_all = gather_tokens(cotangent[0])
    grad_reduce = scatter_rows(t_dot(act_low, grad_all))
    d_gate_up = act_pull(dot_t(grad_all, w_red))[0].astype(jnp.bfloat16)
    grad_expand = scatter_columns(t_dot(normed_mid, d_gate_up), EXPAND_WIDTHS)
    d_normed_mid = scatter_tokens(dot_t(d_gate_up, w_exp))
    unused, mid_pull = jax.vjp(rms_scale, hidden, gain_mid)
    d_hidden_part, d_gain_mid = mid_pull(d_normed_mid)
    d_hidden = grad_val + d_hidden_part
    d_att = gather_tokens(d_hidden.astype(jnp.bfloat16))
    grad_output = scatter_rows(t_dot(mixed_low, d_att))
    d_mixed = dot_t(d_att, w_out).astype(jnp.bfloat16)

    def head_backward(items):
        q_head, d_head, log_total = items
        scores = dot_t(q_head, key) * scale
        probs = jnp.exp(jnp.where(allowed, scores - log_total[:, None], masked_score))
        d_probs = dot_t(d_head, value)
        inner = jnp.sum(probs * d_probs, axis=-1, keepdims=True)
        d_scores = (probs * (d_probs - inner)).astype(jnp.bfloat16)
        return (
            dot(d_scores, key) * scale,
            t_dot(d_scores, q_head) * scale,
            t_dot(probs.astype(jnp.bfloat16), d_head),
        )

    d_query, d_key, d_value = lax.map(
        head_backward,
        (query.transpose(1, 0, 2), d_mixed.reshape(whole, group, HD).transpose(1, 0, 2), log_totals),
    )

    def qk_only(query, key, gain_q, gain_k):
        return qk_prepare(query, key, gain_q, gain_k, cosine, sine)

    unused, qk_pull = jax.vjp(qk_only, query_raw, key_raw, gain_query, gain_key)
    d_query_raw, d_key_raw, d_gain_query, d_gain_key = qk_pull(
        (d_query.transpose(1, 0, 2), jnp.sum(d_key, axis=0)[:, None])
    )
    d_qkv = jnp.concatenate(
        [d_query_raw.reshape(whole, -1), d_key_raw.reshape(whole, -1), jnp.sum(d_value, axis=0)],
        axis=1,
    ).astype(jnp.bfloat16)
    grad_input = scatter_columns(t_dot(normed, d_qkv), IN_WIDTHS)
    d_normed = scatter_tokens(dot_t(d_qkv, w_in))
    unused, in_pull = jax.vjp(rms_scale, x_val, gain_in)
    d_x_part, d_gain_in = in_pull(d_normed)
    input_grad = (d_hidden + d_x_part)[None]
    gain_terms = jnp.concatenate([d_gain_in, d_gain_mid, d_gain_query, d_gain_key])
    grad_gains = lax.psum_scatter(gain_terms, ("dp", "shard"), scatter_dimension=0, tiled=True)
    new_input, mean_input, square_input = adam_step(
        weight_input, grad_input, first_input, second_input, matrix_rate, matrix_decay
    )
    new_output, mean_output, square_output = adam_step(
        weight_output, grad_output, first_output, second_output, matrix_rate, matrix_decay
    )
    new_expand, mean_expand, square_expand = adam_step(
        weight_expand, grad_expand, first_expand, second_expand, matrix_rate, matrix_decay
    )
    new_reduce, mean_reduce, square_reduce = adam_step(
        weight_reduce, grad_reduce, first_reduce, second_reduce, matrix_rate, matrix_decay
    )
    new_gains, mean_gains, square_gains = adam_step(
        gains, grad_gains, first_gains, second_gains, gain_rate, 0.0
    )
    return (
        block_out,
        input_grad,
        new_input,
        new_output,
        new_expand,
        new_reduce,
        new_gains,
        mean_input,
        mean_output,
        mean_expand,
        mean_reduce,
        mean_gains,
        square_input,
        square_output,
        square_expand,
        square_reduce,
        square_gains,
    )


def solution(mesh):
    placed = (
        P("shard", "dp", None),
        P("shard", "dp", None),
        P("shard", None),
        P(("dp", "shard"), None),
        P(("dp", "shard"), None),
        P(("dp", "shard"), None),
        P(("dp", "shard"), None),
        P(("dp", "shard")),
        P(("dp", "shard"), None),
        P(("dp", "shard"), None),
        P(("dp", "shard"), None),
        P(("dp", "shard"), None),
        P(("dp", "shard")),
        P(("dp", "shard"), None),
        P(("dp", "shard"), None),
        P(("dp", "shard"), None),
        P(("dp", "shard"), None),
        P(("dp", "shard")),
    )
    return jax.shard_map(
        body,
        mesh=mesh,
        in_specs=placed,
        out_specs=(
            P("shard", "dp", None),
            P("shard", "dp", None),
            P(("dp", "shard"), None),
            P(("dp", "shard"), None),
            P(("dp", "shard"), None),
            P(("dp", "shard"), None),
            P(("dp", "shard")),
            P(("dp", "shard"), None),
            P(("dp", "shard"), None),
            P(("dp", "shard"), None),
            P(("dp", "shard"), None),
            P(("dp", "shard")),
            P(("dp", "shard"), None),
            P(("dp", "shard"), None),
            P(("dp", "shard"), None),
            P(("dp", "shard"), None),
            P(("dp", "shard")),
        ),
        check_vma=False,
    )
```

time: 2450 us -> 843 us (0.34)
  waiting for transfers between devices: 1880 us -> 325 us
  matrix products: 242 us -> 169 us
  local copies, waits for them, and re-layouts: 72.1 us -> 29.2 us
  other arithmetic: 44.3 us -> 85.3 us
    reduce_scatter x6 -> x5, waiting for transfers between devices: 1730 us -> 132 us  [the longest x4 81.9 us: scatter_tokens(): lax.psum_scatter(partial.astype(jnp.bfloat16), 'dp', scatter_dimension=0,...]
    unnamed x14 -> x15, waiting for transfers between devices: 1.41 us -> 95 us
    dot_general x68 -> x26, matrix products: 242 us -> 169 us  [the longest x10 81.1 us: dot_t(): lax.dot_general(a, b, (((1,), (1,)), ((), ())), preferred_element_type=jn...]
    all_gather x8 -> x6, waiting for transfers between devices: 145 us -> 88.8 us  [the longest x4 73.6 us: gather_tokens(): return lax.all_gather(block, 'dp', axis=0, tiled=True)]
    unnamed x2 -> x3, blocking collectives: 132 us -> 130 us
  transfers between devices with their start and end apart: 14 -> 15, of which waited for: 9 -> 11; matrix products, arithmetic and copies ran while one was open for 7% -> 21% of each run, Pallas kernels for 0% -> 0%
where the time goes in v1:
time: 843 us; the launch traced here: 835 us
  waiting for transfers between devices  325 us (39%)
  blocking collectives  199 us (24%)
  matrix products  169 us (20%)
  other arithmetic  85.3 us (10%)
  local copies, waits for them, and re-layouts  29.2 us (3%)
  between operations  17.7 us (2%)
  starting transfers between devices  8.58 us (1%)
    unnamed x3, blocking collectives  130 us
    unnamed x15, waiting for transfers between devices  95 us
    reduce_scatter x4, waiting for transfers between devices, scatter_tokens(): lax.psum_scatter(partial.astype(jnp.bfloat16), 'dp', scatter_dimension=0,...  81.9 us
    dot_general x10, matrix products, dot_t(): lax.dot_general(a, b, (((1,), (1,)), ((), ())), preferred_element_type=jn...  81.1 us
    all_gather x4, waiting for transfers between devices, gather_tokens(): return lax.all_gather(block, 'dp', axis=0, tiled=True)  73.6 us
    dot_general x8, matrix products, dot(): return jnp.dot(a, b, preferred_element_type=jnp.float32)  52.9 us
    reduce_scatter x1, waiting for transfers between devices, scatter_rows(): lax.psum_scatter(grad.astype(jnp.bfloat16), 'shard', scatter_dimension=0,...  49.9 us
    all_gather x2, blocking collectives, gather_rows(): lax.all_gather(weight.astype(jnp.bfloat16), 'shard', axis=0, tiled=True)  49 us
  transfers between devices with their start and end apart: 15, of which 11 were waited for; matrix products, arithmetic and copies ran while one was open for 21% of the time, Pallas kernels for 0%

profile of v1, /device:TPU:0, one launch (start us, length us, event | category | flops | bytes accessed | tf_op | source)
XLA Modules:
  0.0 835.2 jit_solution(4503726698755689918)
XLA Ops:
  8.2 10.9 %all_to_all.20 = bf16[8,8,512]{2,1,0:T(8,128)(2,1)} all-to-all(bf16[8,8,512]{2,1,0:T(8,128)(2,1)S(1)} %maximum_bitcast_fusion.2), channel_id=1, replica_groups=mesh['dp'=8,'shard'=16] {'dp'}, dimensions={0} | all-to-all | bytes 131072 | tf_op jit(solution)/shard_map/all_to_all | solution.py:107
  23.9 40.9 %all-reduce.6 = f32[288]{0:T(512)S(1)} all-reduce(f32[288]{0:T(512)S(1)} %dynamic-update-slice), channel_id=1, replica_groups=mesh['dp'=8,'shard'=16] {'shard'}, use_global_device_ids=true, to_apply=%add.6 | all-reduce | flops 288 | bytes 2304
  65.1 23.5 %all-reduce.7 = f32[2304]{0:T(1024)S(1)} all-reduce(f32[2304]{0:T(1024)S(1)} %dynamic-update-slice.1), channel_id=1, replica_groups=mesh['dp'=8,'shard'=16] {'dp'}, use_global_device_ids=true, to_apply=%add.7 | all-reduce | flops 2304 | bytes 18432
  91.7 2.0 fusion.52
  96.3 23.7 %all_gather.34 = bf16[256,1024]{1,0:T(8,128)(2,1)} all-gather(bf16[16,1024]{1,0:T(8,128)(2,1)S(1)} %convert_element_type.135), channel_id=1, replica_groups=mesh['dp'=8,'shard'=16] {'shard'}, dimensions={0}, use_global_device_ids=true | all-gather | bytes 557056 | tf_op jit(solution)/shard_map/all_gather | solution.py:113
  120.2 1.9 multiply_cosine_fusion.1
  122.2 5.3 fusion.113
  132.5 2.5 fusion.82
  136.0 1.9 multiply_multiply_fusion
  139.7 52.9 %while.30 = (s32[]{:T(128)}, bf16[2,2048,128]{1,2,0:T(8,128)(2,1)S(1)}, f32[2,2048]{1,0:T(2,128)S(1)}, bf16[2,2048,128]{2,1,0:T(8,128)(2,1)}, bf16[2048,128]{1,0...) while((s32[]{:T(128)}, bf16[2,2048,128]{1,2,0:T(8,128)(2,1)S(1)}, ...), condition=%wide.region_9.10_spmd.clone.clone, body=%wide.region_6.9_spmd.clone.sunk.clone | while | flops 2193618944 | bytes 53051488 | solution.py:212
  139.7 9.3 %fusion.178 = (f32[2048]{0:T(1024)S(1)}, f32[2048,2048]{0,1:T(8,128)}) fusion(bf16[2048,128]{1,0:T(8,128)(2,1)} %get-tuple-element.487, bf16[2,2048,128]{2,1,0:T(8,128)(2,1)} %get-tuple-element.486, s32[]{:T(128)S(6)} %copy.116, s32[2048]{0:T(1024)S(1)} %get-tuple-element.489), kind=kOutput, calls=%fused_computation.196.clone.1.clone | convolution fusion | flops 1098905600 | bytes 17850372 | tf_op jit(solution)/shard_map/while/body/eval_jaxpr/dot_general | solution.py:144
  149.1 8.1 fusion.179
  157.2 8.9 %fusion.180 = bf16[2,2048,128]{1,2,0:T(8,128)(2,1)S(1)} fusion(bf16[2,2048,128]{1,2,0:T(8,128)(2,1)S(1)} %get-tuple-element.477, s32[]{:T(128)S(6)} %copy.116, bf16[2048,128]{1,0:T(8,128)(2,1)} %get-tuple-element.488, f32[2048,2048]{0,1:T(8,128)} %get-tuple-element.434, f32[2048]{0:T(1024)S(1)} %fusion.179, f32[2048]{0:T(1024)S(1)} %get-tuple-element.435), kind=kOutput, calls=%fused_computation.10.clone.1.clone | convolution fusion | flops 1086324736 | bytes 18366468 | tf_op jit(solution)/shard_map/while/body/eval_jaxpr/dot_general | solution.py:140
  166.2 9.3 %fusion.178 = (f32[2048]{0:T(1024)S(1)}, f32[2048,2048]{0,1:T(8,128)}) fusion(bf16[2048,128]{1,0:T(8,128)(2,1)} %get-tuple-element.487, bf16[2,2048,128]{2,1,0:T(8,128)(2,1)} %get-tuple-element.486, s32[]{:T(128)S(6)} %copy.116, s32[2048]{0:T(1024)S(1)} %get-tuple-element.489), kind=kOutput, calls=%fused_computation.196.clone.1.clone | convolution fusion | flops 1098905600 | bytes 17850372 | tf_op jit(solution)/shard_map/while/body/eval_jaxpr/dot_general | solution.py:144
  175.5 8.1 fusion.179
  183.6 8.9 %fusion.180 = bf16[2,2048,128]{1,2,0:T(8,128)(2,1)S(1)} fusion(bf16[2,2048,128]{1,2,0:T(8,128)(2,1)S(1)} %get-tuple-element.477, s32[]{:T(128)S(6)} %copy.116, bf16[2048,128]{1,0:T(8,128)(2,1)} %get-tuple-element.488, f32[2048,2048]{0,1:T(8,128)} %get-tuple-element.434, f32[2048]{0:T(1024)S(1)} %fusion.179, f32[2048]{0:T(1024)S(1)} %get-tuple-element.435), kind=kOutput, calls=%fused_computation.10.clone.1.clone | convolution fusion | flops 1086324736 | bytes 18366468 | tf_op jit(solution)/shard_map/while/body/eval_jaxpr/dot_general | solution.py:140
  193.7 3.3 convolution_convert_fusion.2
  197.9 9.4 %all_to_all.21 = bf16[8,8,768]{2,1,0:T(8,128)(2,1)} all-to-all(bf16[8,8,768]{2,1,0:T(8,128)(2,1)S(1)} %maximum_bitcast_fusion.1), channel_id=1, replica_groups=mesh['dp'=8,'shard'=16] {'dp'}, dimensions={0} | all-to-all | bytes 196608 | tf_op jit(solution)/shard_map/all_to_all | solution.py:107
  207.4 25.2 %reduce-scatter.11.cloned.1.call-done = bf16[256,1024]{1,0:T(8,128)(2,1)} async-done(((bf16[2048,1024]{1,0:T(8,128)(2,1)}), bf16[256,1024]{1,0:T(8,128)(2,1)}) %reduce-scatter.11.cloned.1.call-update) | async-done | bytes 524304 | tf_op jit(solution)/shard_map/reduce_scatter | solution.py:134
  233.9 2.1 multiply_convert_fusion.2
  236.6 25.3 %all_gather.37 = bf16[384,1024]{1,0:T(8,128)(2,1)S(1)} all-gather(bf16[24,1024]{1,0:T(8,128)(2,1)S(1)} %convert_element_type.141), channel_id=1, replica_groups=mesh['dp'=8,'shard'=16] {'shard'}, dimensions={0}, use_global_device_ids=true | all-gather | bytes 835584 | tf_op jit(solution)/shard_map/all_gather | solution.py:113
  261.9 15.2 %all-gather.14.cloned.1.call-done = bf16[8,128,768]{2,1,0:T(8,128)(2,1)} async-done(((bf16[8,8,768]{2,1,0:T(8,128)(2,1)}), bf16[8,128,768]{2,1,0:T(8,128)(2,1)}) %all-gather.14.cloned.1.call-update) | async-done | bytes 1572880 | tf_op jit(solution)/shard_map/all_gather | solution.py:108
  277.1 33.3 %all-gather.12.cloned.1.call-done = bf16[2048,1024]{1,0:T(8,128)(2,1)} async-done(((bf16[256,1024]{1,0:T(8,128)(2,1)}), bf16[2048,1024]{1,0:T(8,128)(2,1)}) %all-gather.12.cloned.1.call-update) | async-done | bytes 4194320 | tf_op jit(solution)/shard_map/all_gather | solution.py:130
  310.4 8.8 %fusion.114 = f32[2048,768]{1,0:T(8,128)} fusion(bf16[2048,1024]{1,0:T(8,128)(2,1)} %all-gather.12.cloned.1.call-done, bf16[1024,768]{1,0:T(8,128)(2,1)} %bitcast.252), kind=kOutput, calls=%fused_computation.204 | convolution fusion | flops 3221225472 | bytes 12058624 | tf_op jit(solution)/shard_map/dot_general | solution.py:140
  319.2 25.0 %all-gather.18.cloned.1.call-done = bf16[1,2048,1024]{2,1,0:T(8,128)(2,1)} async-done(((bf16[1,256,1024]{2,1,0:T(8,128)(2,1)}), bf16[1,2048,1024]{2,1,0:T(8,128)(2,1)}) %all-gather.18.cloned.1.call-update) | async-done | bytes 4194320 | tf_op jit(solution)/shard_map/all_gather | solution.py:130
  344.1 8.7 %fusion.80 = (f32[2048,384]{1,0:T(8,128)S(1)}, f32[2048,384]{1,0:T(8,128)S(1)}, bf16[2048,384]{1,0:T(8,128)(2,1)}) fusion(f32[2048,768]{1,0:T(8,128)} %fusion.114, bf16[384,1024]{1,0:T(8,128)(2,1)S(1)} %all_gather.37, bf16[1,2048,1024]{2,1,0:T(8,128)(2,1)} %all-gather.18.cloned.1.call-done), kind=kOutput, calls=%fused_computation.135 | convolution fusion | flops 1621622784 | bytes 19136512 | tf_op jit(solution)/shard_map/dot_general | solution.py:144
  355.5 5.1 convolution_convert_fusion.3
  360.6 38.1 %reduce-scatter.15.cloned.1.call-done = bf16[256,1024]{1,0:T(8,128)(2,1)} async-done(((bf16[2048,1024]{1,0:T(8,128)(2,1)}), bf16[256,1024]{1,0:T(8,128)(2,1)}) %reduce-scatter.15.cloned.1.call-update) | async-done | bytes 524304 | tf_op jit(solution)/shard_map/reduce_scatter | solution.py:134
  398.7 2.1 fusion.54
  400.9 2.3 fusion.99
  403.2 2.2 copy-done.73
  405.4 4.1 fusion.45
  409.6 9.5 %convolution_convert_fusion.5 = bf16[1024,768]{1,0:T(8,128)(2,1)} fusion(bf16[2048,1024]{1,0:T(8,128)(2,1)} %all-gather.12.cloned.1.call-done, f32[2048,384]{1,0:T(8,128)} %copy-done.76, f32[2048,384]{1,0:T(8,128)} %copy-done.75), kind=kOutput, calls=%fused_computation.73 | convolution fusion | flops 3225157632 | bytes 12058624 | tf_op jit(solution)/shard_map/dot_general | solution.py:148
  419.1 15.2 %all-gather.16.cloned.1.call-done = bf16[2048,1024]{1,0:T(8,128)(2,1)} async-done(((bf16[256,1024]{1,0:T(8,128)(2,1)}), bf16[2048,1024]{1,0:T(8,128)(2,1)}) %all-gather.16.cloned.1.call-update) | async-done | bytes 4194320 | tf_op jit(solution)/shard_map/all_gather | solution.py:130
  434.4 3.5 convolution_convert_fusion.4
  438.5 92.0 %while.31 = (s32[]{:T(128)}, f32[2,2048,128]{1,2,0:T(8,128)}, f32[2,2048,128]{2,1,0:T(8,128)}, f32[2,2048,128]{2,1,0:T(8,128)}, bf16[2,2048,128]{2,1,0:T(8,128)(...) while((s32[]{:T(128)}, f32[2,2048,128]{1,2,0:T(8,128)}, ...), condition=%wide.region_17.18_spmd.clone.clone, body=%wide.region_15.17_spmd.clone.sunk.clone | while | flops 5419563008 | bytes 187230432 | solution.py:251
  438.7 9.2 %fusion.190 = f32[2048,2048]{0,1:T(8,128)} fusion(bf16[2048,128]{1,0:T(8,128)(2,1)} %get-tuple-element.518, bf16[2,2048,128]{2,1,0:T(8,128)(2,1)S(1)} %get-tuple-element.517, s32[]{:T(128)S(6)} %copy.126), kind=kOutput, calls=%fused_computation.30.clone.1.clone | convolution fusion | flops 1073741824 | bytes 17825796 | tf_op jit(solution)/shard_map/while/body/eval_jaxpr/dot_general | solution.py:144
  447.9 10.6 %multiply_reduce_fusion.8 = (f32[2048]{0:T(1024)S(1)}, f32[2048,2048]{0,1:T(8,128)S(1)}) fusion(f32[2048,2048]{0,1:T(8,128)} %fusion.190, f32[2048]{0:T(1024)S(1)} %bitcast.247, bf16[2048,128]{1,0:T(8,128)(2,1)} %get-tuple-element.515, bf16[2,2048,128]{2,1,0:T(8,128)(2,1)} %get-tuple-element.514, s32[]{:T(128)S(6)} %copy.126, ...), kind=kOutput, calls=%fused_computation.17.clone.1.clone | convolution fusion | flops 1107294208 | bytes 34635780 | tf_op jit(solution)/shard_map/while/body/eval_jaxpr/dot_general | solution.py:144
  458.5 11.0 %multiply_convert_fusion.5 = bf16[2048,2048]{0,1:T(8,128)(2,1)} fusion(f32[2048,2048]{0,1:T(8,128)S(1)} %get-tuple-element.456, f32[2048,2048]{0,1:T(8,128)} %fusion.190, f32[2048]{0:T(1024)S(1)} %get-tuple-element.457), kind=kLoop, calls=%fused_computation.16.clone.1.clone | loop fusion | flops 12582912 | bytes 41951232 | tf_op jit(solution)/shard_map/while/body/eval_jaxpr/convert_element_type | solution.py:244
  469.6 2.4 fusion.193
  472.0 6.6 fusion.191
  478.7 4.4 fusion.192
  484.6 9.2 %fusion.190 = f32[2048,2048]{0,1:T(8,128)} fusion(bf16[2048,128]{1,0:T(8,128)(2,1)} %get-tuple-element.518, bf16[2,2048,128]{2,1,0:T(8,128)(2,1)S(1)} %get-tuple-element.517, s32[]{:T(128)S(6)} %copy.126), kind=kOutput, calls=%fused_computation.30.clone.1.clone | convolution fusion | flops 1073741824 | bytes 17825796 | tf_op jit(solution)/shard_map/while/body/eval_jaxpr/dot_general | solution.py:144
  493.8 10.6 %multiply_reduce_fusion.8 = (f32[2048]{0:T(1024)S(1)}, f32[2048,2048]{0,1:T(8,128)S(1)}) fusion(f32[2048,2048]{0,1:T(8,128)} %fusion.190, f32[2048]{0:T(1024)S(1)} %bitcast.247, bf16[2048,128]{1,0:T(8,128)(2,1)} %get-tuple-element.515, bf16[2,2048,128]{2,1,0:T(8,128)(2,1)} %get-tuple-element.514, s32[]{:T(128)S(6)} %copy.126, ...), kind=kOutput, calls=%fused_computation.17.clone.1.clone | convolution fusion | flops 1107294208 | bytes 34635780 | tf_op jit(solution)/shard_map/while/body/eval_jaxpr/dot_general | solution.py:144
  504.4 11.0 %multiply_convert_fusion.5 = bf16[2048,2048]{0,1:T(8,128)(2,1)} fusion(f32[2048,2048]{0,1:T(8,128)S(1)} %get-tuple-element.456, f32[2048,2048]{0,1:T(8,128)} %fusion.190, f32[2048]{0:T(1024)S(1)} %get-tuple-element.457), kind=kLoop, calls=%fused_computation.16.clone.1.clone | loop fusion | flops 12582912 | bytes 41951232 | tf_op jit(solution)/shard_map/while/body/eval_jaxpr/convert_element_type | solution.py:244
  515.4 2.4 fusion.193
  517.8 6.6 fusion.191
  524.5 4.4 fusion.192
  535.6 2.1 fusion.76
  537.7 2.5 multiply_add_fusion.1
  543.3 2.1 convolution_convert_fusion.7
  545.4 3.2 fusion.44
  550.1 6.1 convolution_convert_fusion.6
  556.3 5.6 convolution_convert_fusion.1
  563.6 4.4 convolution_convert_fusion
  570.8 49.9 %reduce-scatter.19.cloned.1.call-done = bf16[16,1024]{1,0:T(8,128)(2,1)} async-done(((bf16[256,1024]{1,0:T(8,128)(2,1)}), bf16[16,1024]{1,0:T(8,128)(2,1)}) %reduce-scatter.19.cloned.1.call-update) | async-done | bytes 32784 | tf_op jit(solution)/shard_map/reduce_scatter | solution.py:124
  622.2 94.3 %all-reduce.15.cloned.1.call-done = (bf16[8,128,512]{2,1,0:T(8,128)(2,1)}, bf16[8,128,768]{2,1,0:T(8,128)(2,1)}) async-done(((bf16[8,128,512]{2,1,0:T(8,128)(2,1)}, bf16[8,128,768]{2,1,0:T(8,128)(2,1)}), (bf16[8,128,512]{2,1,0:T(8,128)(2,1)}, bf16[8,128,768]{2,1,0:T(8,128)(2,1)})) %all-reduce.15.cloned.1.call-update) | async-done | bytes 2621456
  717.9 4.4 all-to-all-start.2
  723.9 4.1 all-to-all-done.2
  728.0 3.4 all-to-all-start.3
  732.2 5.5 all-to-all-done.3
  738.7 18.6 %reduce-scatter.17.cloned.1.call-done = bf16[256,1024]{1,0:T(8,128)(2,1)} async-done(((bf16[2048,1024]{1,0:T(8,128)(2,1)}), bf16[256,1024]{1,0:T(8,128)(2,1)}) %reduce-scatter.17.cloned.1.call-update) | async-done | bytes 524304 | tf_op jit(solution)/shard_map/reduce_scatter | solution.py:134
  758.9 65.5 %all-reduce.11 = f32[2304]{0:T(1024)S(1)} all-reduce(f32[2304]{0:T(1024)S(1)} %pad_maximum_fusion.6), channel_id=11, replica_groups=mesh['dp'=8,'shard'=16] {'dp','shard'}, use_global_device_ids=true, to_apply=%region_32.33.clone | all-reduce | flops 2304 | bytes 18432
  825.1 3.1 fusion.59
  (272 shorter events, 50.0 us)
Async XLA Ops:
  7.2 114.9 %all-gather.10.cloned.1.call-start = ((), (), s32[]{:S(2)}) async-start(), calls=%async_computation.11 | async-start | bytes 1114112 | tf_op jit(solution)/shard_map/all_gather | solution.py:108
  19.1 103.0 %all-gather.8.cloned.1.call-start = ((), (), s32[]{:S(2)}) async-start(), calls=%async_computation.10 | async-start | bytes 4718592 | tf_op jit(solution)/shard_map/all_gather | solution.py:130
  93.7 138.9 %reduce-scatter.11.cloned.1.call-start = ((), (), s32[]{:S(2)}) async-start(), calls=%async_computation.12 | async-start | bytes 4718592 | tf_op jit(solution)/shard_map/reduce_scatter | solution.py:134
  95.4 37.0 %copy-start.67 = (f32[64]{0:T(128)}, f32[64]{0:T(128)S(1)}, u32[]{:S(2)}) copy-start(f32[64]{0:T(128)S(1)} %multiply_power_fusion) | copy-start | bytes 772
  120.0 11.1 %copy-start.63 = (f32[128]{0:T(128)}, f32[128]{0:T(128)S(1)}, u32[]{:S(2)}) copy-start(f32[128]{0:T(128)S(1)} %get-tuple-element.308) | copy-start | bytes 1540
  120.0 16.0 %copy-start.65 = (f32[128]{0:T(128)}, f32[128]{0:T(128)S(1)}, u32[]{:S(2)}) copy-start(f32[128]{0:T(128)S(1)} %get-tuple-element.309) | copy-start | bytes 1540
  120.1 12.4 %copy-start.41 = (f32[2048]{0:T(1024)}, f32[2048]{0:T(1024)S(1)}, u32[]{:S(2)}) copy-start(f32[2048]{0:T(1024)S(1)} %subtract_convert_fusion.1) | copy-start | bytes 24580
  122.1 15.9 %copy-start.15 = (f32[2048,64]{0,1:T(8,128)}, f32[2048,64]{0,1:T(8,128)S(1)}, u32[]{:S(2)}) copy-start(f32[2048,64]{0,1:T(8,128)S(1)} %get-tuple-element.310) | copy-start | bytes 1572868
  122.1 15.9 %copy-start.16 = (f32[2048,64]{0,1:T(8,128)}, f32[2048,64]{0,1:T(8,128)S(1)}, u32[]{:S(2)}) copy-start(f32[2048,64]{0,1:T(8,128)S(1)} %get-tuple-element.311) | copy-start | bytes 1572868
  130.1 7.9 copy-start.39
  130.1 7.9 copy-start.32
  139.7 53.9 %copy-start.20 = (bf16[256,1024]{1,0:T(8,128)(2,1)S(1)}, bf16[256,1024]{1,0:T(8,128)(2,1)}, u32[]{:S(2)}) copy-start(bf16[256,1024]{1,0:T(8,128)(2,1)} %all_gather.34) | copy-start | bytes 1572868
  197.0 35.6 %copy-start.3 = (bf16[1,256,1024]{2,1,0:T(8,128)(2,1)S(1)}, bf16[1,256,1024]{2,1,0:T(8,128)(2,1)}, u32[]{:S(2)}) copy-start(bf16[1,256,1024]{2,1,0:T(8,128)(2,1)} %param.22) | copy-start | bytes 1572868
  197.0 36.9 %copy-start.45 = (f32[1024]{0:T(1024)S(1)}, f32[1024]{0:T(1024)}, u32[]{:S(2)}) copy-start(f32[1024]{0:T(1024)} %get-tuple-element.306) | copy-start | bytes 12292
  197.0 39.6 %copy-start.30 = (f32[24,1024]{1,0:T(8,128)S(1)}, f32[24,1024]{1,0:T(8,128)}, u32[]{:S(2)}) copy-start(f32[24,1024]{1,0:T(8,128)} %param.28) | copy-start | bytes 294916
  197.0 80.1 %all-gather.14.cloned.1.call-start = ((), (), s32[]{:S(2)}) async-start(), calls=%async_computation.14 | async-start | bytes 1671168 | tf_op jit(solution)/shard_map/all_gather | solution.py:108
  207.3 103.1 %all-gather.12.cloned.1.call-start = ((), (), s32[]{:S(2)}) async-start(), calls=%async_computation.13 | async-start | bytes 4718592 | tf_op jit(solution)/shard_map/all_gather | solution.py:130
  233.9 167.0 %copy-start.54 = (f32[256]{0:T(256)}, f32[256]{0:T(256)S(1)}, u32[]{:S(2)}) copy-start(f32[256]{0:T(256)S(1)} %fusion.92) | copy-start | bytes 3076
  236.0 108.2 %all-gather.18.cloned.1.call-start = ((), (), s32[]{:S(2)}) async-start(), calls=%async_computation.20 | async-start | bytes 4718592 | tf_op jit(solution)/shard_map/all_gather | solution.py:130
  236.6 162.2 %reduce-scatter.15.cloned.1.call-start = ((), (), s32[]{:S(2)}) async-start(), calls=%async_computation.16 | async-start | bytes 4718592 | tf_op jit(solution)/shard_map/reduce_scatter | solution.py:134
  261.9 82.2 %copy-start.24 = (bf16[384,1024]{1,0:T(8,128)(2,1)}, bf16[384,1024]{1,0:T(8,128)(2,1)S(1)}, u32[]{:S(2)}) copy-start(bf16[384,1024]{1,0:T(8,128)(2,1)S(1)} %all_gather.37) | copy-start | bytes 2359300
  344.1 11.3 %copy-start.74 = (bf16[8,128,768]{2,1,0:T(8,128)(2,1)S(1)}, bf16[8,128,768]{2,1,0:T(8,128)(2,1)}, u32[]{:S(2)}) copy-start(bf16[8,128,768]{2,1,0:T(8,128)(2,1)} %all-gather.14.cloned.1.call-done) | copy-start | bytes 4718596
  360.5 38.2 %copy-start.5 = (bf16[256,1024]{1,0:T(8,128)(2,1)S(1)}, bf16[256,1024]{1,0:T(8,128)(2,1)}, u32[]{:S(2)}) copy-start(bf16[256,1024]{1,0:T(8,128)(2,1)} %reduce-scatter.11.cloned.1.call-done) | copy-start | bytes 1572868
  360.5 40.3 %copy-start.17 = (bf16[1,256,1024]{2,1,0:T(8,128)(2,1)S(1)}, bf16[1,256,1024]{2,1,0:T(8,128)(2,1)}, u32[]{:S(2)}) copy-start(bf16[1,256,1024]{2,1,0:T(8,128)(2,1)} %param.23) | copy-start | bytes 1572868
  360.6 73.8 %all-gather.16.cloned.1.call-start = ((), (), s32[]{:S(2)}) async-start(), calls=%async_computation.17 | async-start | bytes 4718592 | tf_op jit(solution)/shard_map/all_gather | solution.py:130
  400.8 8.7 %copy-start.61 = (f32[256]{0:T(256)}, f32[256]{0:T(256)S(1)}, u32[]{:S(2)}) copy-start(f32[256]{0:T(256)S(1)} %multiply_multiply_fusion.8) | copy-start | bytes 3076
  403.2 166.0 %reduce-scatter.21.cloned.1.call-start = ((), (), s32[]{:S(2)}) async-start(), calls=%async_computation.21 | async-start | bytes 835584
  409.6 211.0 %reduce-scatter.19.cloned.1.call-start = ((), (), s32[]{:S(2)}) async-start(), calls=%async_computation.19 | async-start | bytes 557056 | tf_op jit(solution)/shard_map/reduce_scatter | solution.py:124
  458.5 11.1 %copy-start.21 = (f32[2,2048,128]{2,1,0:T(8,128)S(1)}, f32[2,2048,128]{2,1,0:T(8,128)}, u32[]{:S(2)}) copy-start(f32[2,2048,128]{2,1,0:T(8,128)} %get-tuple-element.503) | copy-start | bytes 6291460 | tf_op jit(solution)/shard_map/while
  472.0 6.6 copy-start.22
  472.0 6.7 copy-start
  504.4 11.0 %copy-start.21 = (f32[2,2048,128]{2,1,0:T(8,128)S(1)}, f32[2,2048,128]{2,1,0:T(8,128)}, u32[]{:S(2)}) copy-start(f32[2,2048,128]{2,1,0:T(8,128)} %get-tuple-element.503) | copy-start | bytes 6291460 | tf_op jit(solution)/shard_map/while
  517.8 6.6 copy-start.22
  517.8 6.7 copy-start
  530.5 5.0 copy-start.42
  548.6 167.9 %all-reduce.15.cloned.1.call-start = ((), (), s32[]{:S(2)}) async-start(), calls=%async_computation.22 | async-start | bytes 5242880
  550.1 6.2 copy-start.23
  550.1 6.2 copy-start.29
  556.3 201.1 %reduce-scatter.17.cloned.1.call-start = ((), (), s32[]{:S(2)}) async-start(), calls=%async_computation.18 | async-start | bytes 4718592 | tf_op jit(solution)/shard_map/reduce_scatter | solution.py:134
  562.0 263.0 %reduce-scatter.13.cloned.1.call-start = ((), (), s32[]{:S(2)}) async-start(), calls=%async_computation.15 | async-start | bytes 4718592 | tf_op jit(solution)/shard_map/reduce_scatter | solution.py:134
  568.0 52.6 %copy-start.34 = (f32[16,1024]{1,0:T(8,128)S(1)}, f32[16,1024]{1,0:T(8,128)}, u32[]{:S(2)}) copy-start(f32[16,1024]{1,0:T(8,128)} %param.26) | copy-start | bytes 196612
  568.0 52.6 %copy-start.51 = (f32[16,1024]{1,0:T(8,128)S(1)}, f32[16,1024]{1,0:T(8,128)}, u32[]{:S(2)}) copy-start(f32[16,1024]{1,0:T(8,128)} %param.31) | copy-start | bytes 196612
  568.0 163.4 %copy-start.28 = (f32[8,4096]{1,0:T(8,128)S(1)}, f32[8,4096]{1,0:T(8,128)}, u32[]{:S(2)}) copy-start(f32[8,4096]{1,0:T(8,128)} %param.25) | copy-start | bytes 393220
  568.0 163.4 %copy-start.43 = (f32[8,4096]{1,0:T(8,128)S(1)}, f32[8,4096]{1,0:T(8,128)}, u32[]{:S(2)}) copy-start(f32[8,4096]{1,0:T(8,128)} %param.30) | copy-start | bytes 393220
  568.0 163.4 %copy-start.44 = (f32[8,4096]{1,0:T(8,128)S(1)}, f32[8,4096]{1,0:T(8,128)}, u32[]{:S(2)}) copy-start(f32[8,4096]{1,0:T(8,128)} %param.35) | copy-start | bytes 393220
  568.1 169.7 %copy-start.27 = (f32[8,6144]{1,0:T(8,128)S(1)}, f32[8,6144]{1,0:T(8,128)}, u32[]{:S(2)}) copy-start(f32[8,6144]{1,0:T(8,128)} %param.27) | copy-start | bytes 589828
  568.1 169.7 %copy-start.35 = (f32[8,6144]{1,0:T(8,128)S(1)}, f32[8,6144]{1,0:T(8,128)}, u32[]{:S(2)}) copy-start(f32[8,6144]{1,0:T(8,128)} %param.32) | copy-start | bytes 589828
  568.1 169.7 %copy-start.36 = (f32[8,6144]{1,0:T(8,128)S(1)}, f32[8,6144]{1,0:T(8,128)}, u32[]{:S(2)}) copy-start(f32[8,6144]{1,0:T(8,128)} %param.37) | copy-start | bytes 589828
  568.1 189.3 %copy-start.4 = (bf16[1,256,1024]{2,1,0:T(8,128)(2,1)S(1)}, bf16[1,256,1024]{2,1,0:T(8,128)(2,1)}, u32[]{:S(2)}) copy-start(bf16[1,256,1024]{2,1,0:T(8,128)(2,1)} %param.22) | copy-start | bytes 1572868
  568.1 189.3 %copy-start.53 = (f32[1024]{0:T(1024)S(1)}, f32[1024]{0:T(1024)}, u32[]{:S(2)}) copy-start(f32[1024]{0:T(1024)} %copy-done.52) | copy-start | bytes 12292
  568.1 189.3 %copy-start.58 = (f32[256]{0:T(256)S(1)}, f32[256]{0:T(256)}, u32[]{:S(2)}) copy-start(f32[256]{0:T(256)} %copy-done.57) | copy-start | bytes 3076
  568.1 190.8 %copy-start.56 = (f32[1024]{0:T(1024)S(1)}, f32[1024]{0:T(1024)}, u32[]{:S(2)}) copy-start(f32[1024]{0:T(1024)} %get-tuple-element.226) | copy-start | bytes 12292
  568.1 256.2 %copy-start.60 = (f32[256]{0:T(256)S(1)}, f32[256]{0:T(256)}, u32[]{:S(2)}) copy-start(f32[256]{0:T(256)} %copy-done.59) | copy-start | bytes 3076
  568.1 256.2 %copy-start.69 = (f32[18]{0:T(128)S(1)}, f32[18]{0:T(128)}, u32[]{:S(2)}) copy-start(f32[18]{0:T(128)} %param.29) | copy-start | bytes 220
  568.2 256.2 %copy-start.70 = (f32[18]{0:T(128)S(1)}, f32[18]{0:T(128)}, u32[]{:S(2)}) copy-start(f32[18]{0:T(128)} %param.34) | copy-start | bytes 220
  568.2 256.2 %copy-start.71 = (f32[18]{0:T(128)S(1)}, f32[18]{0:T(128)}, u32[]{:S(2)}) copy-start(f32[18]{0:T(128)} %param.39) | copy-start | bytes 220
  568.2 256.9 %copy-start.6 = (bf16[256,1024]{1,0:T(8,128)(2,1)S(1)}, bf16[256,1024]{1,0:T(8,128)(2,1)}, u32[]{:S(2)}) copy-start(bf16[256,1024]{1,0:T(8,128)(2,1)} %reduce-scatter.11.cloned.1.call-done) | copy-start | bytes 1572868
  568.2 256.9 %copy-start.18 = (bf16[1,256,1024]{2,1,0:T(8,128)(2,1)S(1)}, bf16[1,256,1024]{2,1,0:T(8,128)(2,1)}, u32[]{:S(2)}) copy-start(bf16[1,256,1024]{2,1,0:T(8,128)(2,1)} %param.23) | copy-start | bytes 1572868
  568.2 256.8 %copy-start.19 = (bf16[256,1024]{1,0:T(8,128)(2,1)S(1)}, bf16[256,1024]{1,0:T(8,128)(2,1)}, u32[]{:S(2)}) copy-start(bf16[256,1024]{1,0:T(8,128)(2,1)} %reduce-scatter.15.cloned.1.call-done) | copy-start | bytes 1572868
  568.2 256.8 %copy-start.46 = (f32[1024]{0:T(1024)S(1)}, f32[1024]{0:T(1024)}, u32[]{:S(2)}) copy-start(f32[1024]{0:T(1024)} %get-tuple-element.306) | copy-start | bytes 12292
  568.2 256.8 %copy-start.55 = (f32[256]{0:T(256)S(1)}, f32[256]{0:T(256)}, u32[]{:S(2)}) copy-start(f32[256]{0:T(256)} %copy-done.54) | copy-start | bytes 3076
  568.2 256.8 %copy-start.62 = (f32[256]{0:T(256)S(1)}, f32[256]{0:T(256)}, u32[]{:S(2)}) copy-start(f32[256]{0:T(256)} %copy-done.61) | copy-start | bytes 3076
  717.9 10.1 %all-to-all-start.2 = ((bf16[8,8,512]{2,1,0:T(8,128)(2,1)}), bf16[8,8,512]{2,1,0:T(8,128)(2,1)S(1)}, u32[]{:S(2)}, u32[]{:S(2)}) async-start(bf16[8,8,512]{2,1,0:T(8,128)(2,1)} %constant_dynamic-slice_fusion.2), calls=%async_computation.6 | async-start | bytes 131072 | tf_op jit(solution)/shard_map/all_to_all | solution.py:120
  728.0 9.8 %all-to-all-start.3 = ((bf16[8,8,768]{2,1,0:T(8,128)(2,1)}), bf16[8,8,768]{2,1,0:T(8,128)(2,1)S(1)}, u32[]{:S(2)}, u32[]{:S(2)}) async-start(bf16[8,8,768]{2,1,0:T(8,128)(2,1)} %constant_dynamic-slice_fusion.1), calls=%async_computation.8 | async-start | bytes 196608 | tf_op jit(solution)/shard_map/all_to_all | solution.py:120
  (33 other events, 76.3 us)
Sparse Core Ops, SparseCore 0:
  19.3 42.8 all-gather.9
  93.8 25.6 all-gather.7
  197.1 35.4 reduce-scatter.10
  234.6 42.4 all-gather.13
  278.6 31.7 all-gather.11
  312.0 32.1 all-gather.17
  360.7 37.9 reduce-scatter.14
  403.3 31.0 all-gather.15
  437.6 72.3 reduce-scatter.20
  548.7 71.9 reduce-scatter.18
  624.4 91.9 all-reduce.14
  718.7 38.6 reduce-scatter.16
  759.8 37.4 reduce-scatter.12

commit v2 on v1

v2 whole, which is shorter than its diff:
```python
import math

import jax
import jax.numpy as jnp
from jax import lax
from jax.experimental import pallas as pl
from jax.experimental.pallas import tpu as pltpu
from jax.sharding import PartitionSpec as P

D = 1024
H = 16
KV = 8
HD = 128
FF = 3072
STEP = 10


norm_eps = 1e-06
rope_base = 1000000.0
beta_one = 0.9
beta_two = 0.95
adam_eps = 1e-08
matrix_rate = 0.1
gain_rate = 0.5
matrix_decay = 0.1
masked_score = -1e30


def rms_scale(values, gain):
    return values * lax.rsqrt(jnp.mean(values * values, axis=-1, keepdims=True) + norm_eps) * gain


def rope_tables(positions, width):
    half = width // 2
    freq = rope_base ** (-(2.0 * jnp.arange(half, dtype=jnp.float32)) / width)
    angle = positions.astype(jnp.float32)[:, None] * freq[None, :]
    return (jnp.cos(angle), jnp.sin(angle))


def rotate(values, cosine, sine):
    half = values.shape[-1] // 2
    first = values[..., :half]
    second = values[..., half:]
    cos_b = cosine[:, None, :]
    sin_b = sine[:, None, :]
    return jnp.concatenate(
        [first * cos_b - second * sin_b, second * cos_b + first * sin_b], axis=-1
    )


def seq_layout(lengths, count):
    ends = jnp.cumsum(lengths)
    starts = ends - lengths
    index = jnp.arange(count, dtype=jnp.int32)
    segment = jnp.sum((index[:, None] >= ends[None, :]).astype(jnp.int32), axis=1)
    onehot = (segment[:, None] == jnp.arange(lengths.shape[0], dtype=jnp.int32)[None, :]).astype(
        jnp.int32
    )
    position = index - jnp.sum(onehot * starts[None, :], axis=1)
    return (segment, position)


def adam_step(weight, grad, first, second, rate, decay):
    first_new = beta_one * first + (1.0 - beta_one) * grad
    second_new = beta_two * second + (1.0 - beta_two) * grad * grad
    fix_one = 1.0 - beta_one**STEP
    fix_two = 1.0 - beta_two**STEP
    direction = first_new / fix_one / (jnp.sqrt(second_new / fix_two) + adam_eps)
    return (weight - rate * (direction + decay * weight), first_new, second_new)


MESH = pl.DeviceIdType.MESH
F32 = jnp.float32
BF = jnp.bfloat16
VMEM = pl.BlockSpec(memory_space=pltpu.VMEM)
IN_COLS = (H + 2 * KV) * HD // 8
EXP_COLS = 2 * FF // 8
RED_ROWS = 32


def dot(a, b):
    return jnp.dot(a, b, preferred_element_type=F32)


def dot_t(a, b):
    return lax.dot_general(a, b, (((1,), (1,)), ((), ())), preferred_element_type=F32)


def t_dot(a, b):
    return lax.dot_general(a, b, (((0,), (0,)), ((), ())), preferred_element_type=F32)


def place():
    dp = lax.axis_index("dp")
    shard = lax.axis_index("shard")
    return dp // 2, lax.rem(dp, 2), shard // 4, lax.rem(shard, 4)


def device(z, core, x, y):
    return (lax.rem(z, 4) * 2 + core, lax.rem(x, 4) * 4 + lax.rem(y, 4))


def line_peers():
    z, core, x, y = place()
    return [device(z, 1 - core, x, y), device(z + 1, core, x, y), device(z + 3, core, x, y)]


def plane_peers():
    z, core, x, y = place()
    return [device(z, core, x + k, y) for k in (1, 2, 3)] + [
        device(z, core, x, y + k) for k in (1, 2, 3)
    ]


def dp_peers():
    dp = lax.axis_index("dp")
    shard = lax.axis_index("shard")
    return [(lax.rem(dp + k, 8), shard) for k in range(1, 8)]


def meet(peers):
    barrier = pltpu.get_barrier_semaphore()
    for peer in peers:
        pl.semaphore_signal(barrier, inc=1, device_id=peer, device_id_type=MESH)
    pl.semaphore_wait(barrier, len(peers))


def remote(src, dst, send, recv, peer):
    return pltpu.make_async_remote_copy(
        src_ref=src, dst_ref=dst, send_sem=send, recv_sem=recv, device_id=peer, device_id_type=MESH
    )


class LineGather:
    sems = 13

    def __init__(self, buf, send, recv):
        z, core, x, y = place()
        me, right, far, left = (lax.rem(z + k, 4) * 2 + core for k in range(4))
        to_right, to_left = device(z + 1, core, x, y), device(z + 3, core, x, y)
        sibling = device(z, 1 - core, x, y)
        plan = [
            (me, 0, to_right),
            (me, 1, to_right),
            (left, 0, to_right),
            (me, 1, to_left),
            (me, 0, to_left),
            (right, 1, to_left),
            (me, None, sibling),
            (left, 0, sibling),
            (right, 1, sibling),
            (left, 1, sibling),
            (right, 0, sibling),
            (far, 0, sibling),
            (far, 1, sibling),
        ]
        self.copies = []
        for k, (slot, half, peer) in enumerate(plan):
            ref = buf.at[slot] if half is None else buf.at[slot, half]
            self.copies.append(remote(ref, ref, send.at[k], recv.at[k], peer))

    def start(self, *which):
        for k in which:
            self.copies[k].start()

    def wait(self, *which):
        for k in which:
            self.copies[k].wait_recv()

    def begin(self):
        self.start(6, 0, 3, 1, 4)

    def pass_on(self):
        self.wait(0)
        self.start(2, 7)
        self.wait(3)
        self.start(5, 8)

    def second(self):
        self.wait(1)
        self.start(9)
        self.wait(4)
        self.start(10)

    def third(self):
        self.wait(2)
        self.start(11)
        self.wait(5)
        self.start(12)

    def sent(self):
        for copy in self.copies:
            copy.wait_send()


class PlaneGather:
    sems = 12

    def __init__(self, buf, send, recv):
        z, core, x, y = place()
        half = buf.shape[3] // 2
        low, high = pl.ds(0, half), pl.ds(half, half)
        self.copies = []
        refs = (
            (buf.at[x, y, :, low], 0),
            (buf.at[x, y, :, high], 1),
            (buf.at[:, y, :, low], 1),
            (buf.at[x, :, :, high], 0),
        )
        k = 0
        for ref, along_y in refs:
            for step in (1, 2, 3):
                peer = device(z, core, x, y + step) if along_y else device(z, core, x + step, y)
                self.copies.append(remote(ref, ref, send.at[k], recv.at[k], peer))
                k += 1

    def begin(self):
        for k in (0, 3, 1, 4, 2, 5):
            self.copies[k].start()

    def pass_on(self):
        for k in (0, 1, 2):
            self.copies[k].wait_recv()
        for k in (6, 7, 8):
            self.copies[k].start()
        for k in (3, 4, 5):
            self.copies[k].wait_recv()
        for k in (9, 10, 11):
            self.copies[k].start()

    def end(self):
        for k in range(6, 12):
            self.copies[k].wait_recv()

    def sent(self):
        for copy in self.copies:
            copy.wait_send()


class PlaneScatter:
    sems = 12

    def __init__(self, parts, got1, mid, got2, send, recv):
        z, core, x, y = place()
        self.parts, self.got1, self.mid, self.got2 = parts, got1, mid, got2
        half = parts.shape[3] // 2
        self.cols = (pl.ds(0, half), pl.ds(half, half))
        self.x, self.y = x, y
        self.copies = []
        k = 0
        for side in (0, 1):
            for step in (1, 2, 3):
                if side == 0:
                    ref = parts.at[:, lax.rem(y + step, 4), :, self.cols[0]]
                    peer = device(z, core, x, y + step)
                else:
                    ref = parts.at[lax.rem(x + step, 4), :, :, self.cols[1]]
                    peer = device(z, core, x + step, y)
                self.copies.append(remote(ref, got1.at[side, step - 1], send.at[k], recv.at[k], peer))
                k += 1
        for side in (0, 1):
            for step in (1, 2, 3):
                if side == 0:
                    ref = mid.at[0, lax.rem(x + step, 4)]
                    peer = device(z, core, x + step, y)
                else:
                    ref = mid.at[1, lax.rem(y + step, 4)]
                    peer = device(z, core, x, y + step)
                self.copies.append(remote(ref, got2.at[side, step - 1], send.at[k], recv.at[k], peer))
                k += 1

    def begin(self):
        for k in (0, 3, 1, 4, 2, 5):
            self.copies[k].start()

    def pass_on(self):
        for side in (0, 1):
            for k in range(3 * side, 3 * side + 3):
                self.copies[k].wait_recv()
            for j in range(4):
                if side == 0:
                    own = self.parts[j, self.y, :, self.cols[0]]
                else:
                    own = self.parts[self.x, j, :, self.cols[1]]
                total = own.astype(F32)
                for k in range(3):
                    total += self.got1[side, k, j].astype(F32)
                self.mid[side, j] = total.astype(BF)
            for k in range(6 + 3 * side, 9 + 3 * side):
                self.copies[k].start()

    def end(self, out):
        for side in (0, 1):
            for k in range(6 + 3 * side, 9 + 3 * side):
                self.copies[k].wait_recv()
            total = self.mid[side, self.x if side == 0 else self.y].astype(F32)
            for k in range(3):
                total += self.got2[side, k].astype(F32)
            out[:, self.cols[side]] = total

    def sent(self):
        for copy in self.copies:
            copy.wait_send()


def plane_scatter_scratch(rows, width):
    half = width // 2
    return [
        pltpu.VMEM((2, 3, 4, rows, half), BF),
        pltpu.VMEM((2, 4, rows, half), BF),
        pltpu.VMEM((2, 3, rows, half), BF),
        pltpu.SemaphoreType.DMA((12,)),
        pltpu.SemaphoreType.DMA((12,)),
    ]


class LineScatter:
    sems = 10

    def __init__(self, keep, give, took, out_z, in_z, send, recv):
        z, core, x, y = place()
        self.keep, self.took, self.out_z, self.in_z = keep, took, out_z, in_z
        to_right, to_left = device(z + 1, core, x, y), device(z + 3, core, x, y)
        sibling = device(z, 1 - core, x, y)
        self.swap = [remote(give.at[k], took.at[k], send.at[k], recv.at[k], sibling) for k in range(4)]
        self.copies = [
            remote(
                out_z.at[k], in_z.at[k], send.at[4 + k], recv.at[4 + k], to_right if k < 3 else to_left
            )
            for k in range(6)
        ]

    def give(self, offset):
        self.swap[offset].start()

    def take(self, offset):
        self.swap[offset].wait_recv()

    def half(self, offset, part):
        return self.keep[offset, part] + self.took[offset, part].astype(F32)

    def push(self, k, value):
        self.out_z[k] = value.astype(BF)
        self.copies[k].start()

    def far(self):
        self.take(2)
        self.push(0, self.half(2, 0))
        self.push(3, self.half(2, 1))

    def near(self):
        self.take(1)
        self.push(1, self.half(1, 1))
        self.take(3)
        self.push(4, self.half(3, 0))

    def last(self):
        self.copies[0].wait_recv()
        self.push(2, self.half(1, 0) + self.in_z[0].astype(F32))
        self.copies[3].wait_recv()
        self.push(5, self.half(3, 1) + self.in_z[3].astype(F32))

    def result(self):
        self.take(0)
        self.copies[1].wait_recv()
        self.copies[4].wait_recv()
        self.copies[2].wait_recv()
        first = self.half(0, 0) + self.in_z[4].astype(F32) + self.in_z[2].astype(F32)
        self.copies[5].wait_recv()
        second = self.half(0, 1) + self.in_z[1].astype(F32) + self.in_z[5].astype(F32)
        return first, second

    def sent(self):
        for copy in self.swap + self.copies:
            copy.wait_send()


def line_scatter_scratch(rows, width):
    return [
        pltpu.VMEM((4, 2, rows, width), F32),
        pltpu.VMEM((4, 2, rows, width), BF),
        pltpu.VMEM((4, 2, rows, width), BF),
        pltpu.VMEM((6, rows, width), BF),
        pltpu.VMEM((6, rows, width), BF),
        pltpu.SemaphoreType.DMA((10,)),
        pltpu.SemaphoreType.DMA((10,)),
    ]


def to_send(w_in, w_exp, gains, out):
    col = 0
    for ref, start, width in (
        (w_in, 0, 256),
        (w_in, H * HD, 128),
        (w_in, (H + KV) * HD, 128),
        (w_exp, 0, 384),
        (w_exp, FF, 384),
    ):
        for j in range(8):
            out[j, :, col : col + width] = ref[:, start + j * width : start + (j + 1) * width]
        col += width
    for j in range(8):
        out[j, :, col : col + 128] = gains[...]


def spread_gains(gbuf):
    wide = 128 * 18
    held = gbuf[:, :, :, 0:128].reshape(128, 128)
    n = lax.broadcasted_iota(jnp.int32, (128, wide), 1)
    r = lax.broadcasted_iota(jnp.int32, (128, wide), 0)
    nf = n.astype(F32)
    within = nf - 18.0 * jnp.floor((nf + 0.5) * (1.0 / 18.0))
    pick = jnp.where(within == r.astype(F32), 1.0, 0.0)
    spread = jnp.dot(held, pick, precision=lax.Precision.HIGHEST, preferred_element_type=F32)
    first = ((r & 7) * 16 + (r >> 3)) * 18
    return jnp.sum(jnp.where((n >= first) & (n < first + 18), spread, 0.0), axis=0, keepdims=True)


def fill_order(perm):
    def block(i, carry):
        n = lax.broadcasted_iota(jnp.int32, (128, D), 0)
        k = lax.broadcasted_iota(jnp.int32, (128, D), 1)
        goal = (n >> 3) * 64 + i * 8 + (n & 7)
        perm[pl.ds(pl.multiple_of(i * 128, 128), 128), :] = jnp.where(k == goal, 1.0, 0.0).astype(BF)
        return carry

    lax.fori_loop(0, 8, block, 0)


def normed_rows(values):
    return lax.rsqrt(jnp.mean(values * values, axis=-1, keepdims=True) + norm_eps)


def front_kernel(
    x_ref, w_in_ref, w_exp_ref, gains_ref, cos_ref, sin_ref, w_out_ref, w_red_ref,
    a_ref, raw_ref, q_ref, k_ref, v_ref, win_ref, wexp_ref, gain_ref, wout_all, wred_all,
    xall, wsend, wgot, gbuf, perm,
    line_send, line_recv, cols_send, cols_recv, win_send, win_recv, g_send, g_recv,
    o_send, o_recv, r_send, r_recv,
):
    z, core, x, y = place()
    dp = lax.axis_index("dp")
    peers = dp_peers()
    xall[dp] = x_ref[...].reshape(2, 128, D)
    to_send(w_in_ref, w_exp_ref, gains_ref, wsend)
    wout_all[x, y] = w_out_ref[...].astype(BF)
    wred_all[x, y] = jnp.concatenate([w_red_ref[...], jnp.zeros((8, D), F32)], axis=0).astype(BF)
    meet(peers + plane_peers())
    cols = [
        remote(
            wsend.at[lax.rem(dp + k, 8)], wgot.at[dp], cols_send.at[k - 1], cols_recv.at[k - 1], peers[k - 1]
        )
        for k in range(1, 8)
    ]
    for copy in cols:
        copy.start()
    line = LineGather(xall, line_send, line_recv)
    line.begin()
    wgot[dp] = wsend[dp]
    fill_order(perm)
    for copy in cols:
        copy.wait_recv()
    mine = wgot[:, :, 0 : IN_COLS + EXP_COLS].reshape(64, IN_COLS + EXP_COLS).astype(BF)
    win_ref[x, y] = mine[:, 0:IN_COLS]
    wexp_ref[...] = mine[:, IN_COLS:]
    own_gains = wgot[:, 0, IN_COLS + EXP_COLS :]
    gbuf[x, y, :, 0:128] = own_gains
    gbuf[x, y, :, 128:256] = own_gains
    plane_g = PlaneGather(gbuf, g_send, g_recv)
    plane_w = PlaneGather(win_ref, win_send, win_recv)
    plane_g.begin()
    plane_w.begin()
    plane_o = PlaneGather(wout_all, o_send, o_recv)
    plane_r = PlaneGather(wred_all, r_send, r_recv)
    plane_o.begin()
    plane_r.begin()
    plane_g.pass_on()
    line.pass_on()
    plane_w.pass_on()
    plane_g.end()
    gain_ref[...] = jnp.broadcast_to(spread_gains(gbuf), gain_ref.shape)
    plane_w.end()

    def rows_of(block, carry):
        rows = pl.ds(pl.multiple_of(block * 256, 256), 256)
        values = xall[block].reshape(256, D).astype(F32)
        a = (values * normed_rows(values) * gain_ref[0:1, 0:D]).astype(BF)
        a = dot(a, perm[...]).astype(BF)
        a_ref[rows, :] = a
        qkv = dot(a, win_ref[...].reshape(D, IN_COLS))
        raw_ref[rows, :] = qkv[:, 0:384]
        for part in range(3):
            u = qkv[:, part * HD : (part + 1) * HD]
            start = 2 * D + (HD if part == 2 else 0)
            u = u * normed_rows(u) * gain_ref[0:1, start : start + HD]
            u = (u * cos_ref[rows, :] + pltpu.roll(u, HD // 2, 1) * sin_ref[rows, :]).astype(BF)
            if part < 2:
                q_ref[rows, part * HD : (part + 1) * HD] = u
            else:
                k_ref[rows, :] = u
        v_ref[rows, :] = qkv[:, 384:512].astype(BF)
        return carry

    def chip(offset):
        first = lax.rem(z + offset, 4) * 2
        lax.fori_loop(first, first + 2, rows_of, 0)

    line.wait(6)
    chip(0)
    line.second()
    plane_o.pass_on()
    plane_r.pass_on()
    line.wait(7, 8, 9, 10)

    def near(t, carry):
        first = lax.rem(z + 1 + 2 * (t // 2), 4) * 2
        return rows_of(first + lax.rem(t, 2), carry)

    lax.fori_loop(0, 4, near, 0)
    line.third()
    line.wait(11, 12)
    chip(2)
    line.sent()
    plane_o.end()
    plane_r.end()
    plane_o.sent()
    plane_r.sent()
    plane_g.sent()
    plane_w.sent()
    for copy in cols:
        copy.wait_send()


def front(x, w_in, w_exp, gains, cos, sin, w_out, w_red):
    sh = jax.ShapeDtypeStruct
    return pl.pallas_call(
        front_kernel,
        out_shape=(
            sh((2048, D), BF),
            sh((2048, 384), F32),
            sh((2048, 256), BF),
            sh((2048, 128), BF),
            sh((2048, 128), BF),
            sh((4, 4, 64, IN_COLS), BF),
            sh((64, EXP_COLS), BF),
            sh((8, 2304), F32),
            sh((4, 4, 16, D), BF),
            sh((4, 4, RED_ROWS, D), BF),
        ),
        in_specs=[VMEM] * 8,
        out_specs=[VMEM] * 10,
        scratch_shapes=[
            pltpu.VMEM((8, 2, 128, D), BF),
            pltpu.VMEM((8, 8, IN_COLS + EXP_COLS + 128), F32),
            pltpu.VMEM((8, 8, IN_COLS + EXP_COLS + 128), F32),
            pltpu.VMEM((4, 4, 8, 256), F32),
            pltpu.VMEM((D, D), BF),
        ]
        + [pltpu.SemaphoreType.DMA((n,)) for n in (13, 13, 7, 7, 12, 12, 12, 12, 12, 12, 12, 12)],
        compiler_params=pltpu.CompilerParams(
            collective_id=1, has_side_effects=True, vmem_limit_bytes=56 * 2**20
        ),
        name="front",
    )(x, w_in, w_exp, gains, cos, sin, w_out, w_red)


def rope_full(lengths, whole):
    segment, position = seq_layout(lengths, whole)
    cosine, sine = rope_tables(position, HD)
    return (
        segment,
        jnp.concatenate([cosine, cosine], axis=1),
        jnp.concatenate([-sine, sine], axis=1),
    )


def padded_gains(gains):
    return jnp.broadcast_to(jnp.pad(gains, (0, 128 - gains.shape[0]))[None], (8, 128))


SCORE = HD**-0.5 * math.log2(math.e)
BLOCK = 256
BIG = 30000.0


def extra_columns(segment):
    lane = jnp.arange(128)[None, :]
    same = segment[:, None] == lane
    q_extra = jnp.where((lane < 4) & ~same, -BIG, 0.0).astype(BF)
    k_extra = jnp.where(lane < 4, same.astype(F32), jnp.where(lane < 7, 1.0, 0.0)).astype(BF)
    v_extra = jnp.broadcast_to((lane < 3).astype(BF), (segment.shape[0], 128))
    return q_extra, k_extra, v_extra


def block_rows(i):
    return pl.ds(pl.multiple_of(i * BLOCK, BLOCK), BLOCK)


def wide_rows(i):
    return pl.ds(pl.multiple_of(i * 2 * BLOCK, 2 * BLOCK), 2 * BLOCK)


def attend_block(i, q_ref, k_ref, v_ref, qx_ref, kx_ref, vx_ref, o_ref, lse_ref, acc, qs):
    rows = block_rows(i)
    for h in range(2):
        qs[h * BLOCK : (h + 1) * BLOCK, 0:HD] = q_ref[rows, h * HD : (h + 1) * HD]
        qs[h * BLOCK : (h + 1) * BLOCK, HD:] = qx_ref[rows, :]

    def keys(kr):
        return (
            jnp.concatenate([k_ref[kr, :], kx_ref[kr, :]], axis=1),
            jnp.concatenate([v_ref[kr, :], vx_ref[kr, :]], axis=1),
        )

    kk, vv = keys(rows)
    query = lax.broadcasted_iota(jnp.int32, (2 * BLOCK, BLOCK), 0) & (BLOCK - 1)
    index = lax.broadcasted_iota(jnp.int32, (2 * BLOCK, BLOCK), 1)
    e = jnp.where(index <= query, jnp.exp2(dot_t(qs[...], kk) * SCORE), 0.0)
    acc[...] = dot(e.astype(BF), vv)

    def step(kr):
        kk, vv = keys(kr)
        acc[...] += dot(jnp.exp2(dot_t(qs[...], kk) * SCORE).astype(BF), vv)

    def wide(j, carry):
        step(wide_rows(j))
        return carry

    def narrow(j, carry):
        step(block_rows(j))
        return carry

    lax.fori_loop(0, i // 2, wide, 0)
    lax.fori_loop(i // 2 * 2, i, narrow, 0)
    total = acc[:, HD : HD + 1]
    out = acc[:, 0:HD] * (1.0 / total)
    lse = jnp.log2(total) * (1.0 / SCORE)
    for h in range(2):
        part = slice(h * BLOCK, (h + 1) * BLOCK)
        o_ref[rows, h * HD : (h + 1) * HD] = out[part].astype(BF)
        lse_ref[rows, h : h + 1] = lse[part]


def attention_kernel(
    q_ref, k_ref, v_ref, qx_ref, kx_ref, vx_ref, wexp_ref, dy_ref,
    o_ref, lse_ref, wexp_all, dy_all,
    acc, qs, line_send, line_recv, w_send, w_recv,
):
    z, core, x, y = place()
    wexp_all[x, y] = wexp_ref[...]
    dy_all[lax.axis_index("dp")] = dy_ref[...].reshape(2, 128, D)
    meet(line_peers() + plane_peers())
    plane = PlaneGather(wexp_all, w_send, w_recv)
    line = LineGather(dy_all, line_send, line_recv)
    plane.begin()
    line.begin()

    def block(t, carry):
        attend_block(7 - t, q_ref, k_ref, v_ref, qx_ref, kx_ref, vx_ref, o_ref, lse_ref, acc, qs)

        @pl.when(t == 0)
        def _():
            plane.pass_on()

        @pl.when(t == 1)
        def _():
            line.pass_on()

        @pl.when(t == 3)
        def _():
            line.second()

        return carry

    lax.fori_loop(0, 8, block, 0)
    line.third()
    plane.end()
    line.wait(6, 7, 8, 9, 10, 11, 12)
    plane.sent()
    line.sent()


def attention(q, k, v, qx, kx, vx, wexp, dy):
    sh = jax.ShapeDtypeStruct
    return pl.pallas_call(
        attention_kernel,
        out_shape=(sh((2048, 256), BF), sh((2048, 128), F32), sh((4, 4, 64, EXP_COLS), BF), sh((8, 2, 128, D), BF)),
        in_specs=[VMEM] * 8,
        out_specs=[VMEM] * 4,
        scratch_shapes=[pltpu.VMEM((2 * BLOCK, 256), F32), pltpu.VMEM((2 * BLOCK, 256), BF)]
        + [pltpu.SemaphoreType.DMA((n,)) for n in (13, 13, 12, 12)],
        compiler_params=pltpu.CompilerParams(
            collective_id=2, has_side_effects=True, vmem_limit_bytes=56 * 2**20
        ),
        name="attention",
    )(q, k, v, qx, kx, vx, wexp, dy)


def rms_back(h, r, gain, d):
    dg = d * gain
    return r * dg - h * (r * r * r) * jnp.mean(h * dg, axis=-1, keepdims=True)


def unorder(values, perm):
    high = values.astype(BF)
    low = (values - high.astype(F32)).astype(BF)
    return dot_t(high, perm) + dot_t(low, perm)


def mid_kernel(
    x_ref, o_ref, wout_ref, wexp_ref, wred_ref, dy_ref, gain_ref,
    hid_ref, dhid_ref, act_ref, do_ref, gred_ref, gexp_ref, gout_ref, dgain_ref, wred_out,
    perm, ball, datt, dgu, dbk,
    keep, give, took, out_z, in_z,
    s1_send, s1_recv, b_send, b_recv, s2_send, s2_recv, d_send, d_recv,
):
    z, core, x, y = place()
    dp = lax.axis_index("dp")
    meet(line_peers())
    wout = wout_ref[...].reshape(256, D)
    scatter = LineScatter(keep, give, took, out_z, in_z, s1_send, s1_recv)

    def block_of(offset, own):
        return lax.rem(z + offset, 4) * 2 + (core if own else 1 - core)

    for offset in (2, 1, 3, 0):
        give[offset] = dot(o_ref[block_rows(block_of(offset, False)), :], wout).astype(BF).reshape(2, 128, D)
        scatter.give(offset)
        keep[offset] = dot(o_ref[block_rows(block_of(offset, True)), :], wout).reshape(2, 128, D)
    scatter.far()
    scatter.near()
    fill_order(perm)
    wred_out[...] = (
        wred_ref[...].astype(F32)[:, :, 0:24, :].reshape(FF // 8, D).astype(BF)
    )
    scatter.last()
    first, second = scatter.result()
    hid_ref[...] = x_ref[...].astype(F32) + jnp.concatenate([first, second], axis=0)
    gain = gain_ref[0:1, D : 2 * D]
    hid = hid_ref[...]
    b = (hid * normed_rows(hid) * gain).astype(BF)
    ball[dp] = dot(b, perm[...]).astype(BF).reshape(2, 128, D)
    line = LineGather(ball, b_send, b_recv)
    line.begin()
    scatter.sent()
    scatter = LineScatter(keep, give, took, out_z, in_z, s2_send, s2_recv)

    def mlp(block):
        rows = block_rows(block)
        wexp = wexp_ref[...].reshape(D, EXP_COLS)
        gu = dot(ball[block].reshape(256, D), wexp)
        gate, up = gu[:, : FF // 8], gu[:, FF // 8 :]
        sig = 1.0 / (1.0 + jnp.exp(-gate))
        silu = gate * sig
        act_ref[rows, :] = (silu * up).astype(BF)
        d_act = dot_t(dy_ref[block].reshape(256, D), wred_out[...])
        d_gate = d_act * up * (sig * (1.0 + gate * (1.0 - sig)))
        dgu[rows, 0 : FF // 8] = d_gate.astype(BF)
        dgu[rows, FF // 8 :] = (d_act * silu).astype(BF)
        return dot_t(dgu[rows, :], wexp).reshape(2, 128, D)

    def chip(offset):
        give[offset] = mlp(block_of(offset, False)).astype(BF)
        scatter.give(offset)
        keep[offset] = mlp(block_of(offset, True))

    line.wait(6)
    chip(0)
    line.pass_on()
    line.second()
    line.wait(7, 8, 9, 10)
    chip(1)
    chip(3)
    scatter.near()
    line.third()
    line.wait(11, 12)
    chip(2)
    scatter.far()
    gred_ref[...] = jnp.concatenate(
        [
            t_dot(act_ref[...], dy_ref[...].reshape(2048, D)).reshape(4, 4, 24, D),
            jnp.zeros((4, 4, 8, D), F32),
        ],
        axis=2,
    ).astype(BF)
    gexp_ref[...] = t_dot(ball[...].reshape(2048, D), dgu[...]).astype(BF).reshape(4, 4, 64, EXP_COLS)
    scatter.last()
    first, second = scatter.result()
    d_b = unorder(jnp.concatenate([first, second], axis=0), perm[...])
    hid = hid_ref[...]
    r = normed_rows(hid)
    dgain_ref[...] = jnp.broadcast_to(jnp.sum(d_b * hid * r, axis=0, keepdims=True), (8, D))
    d_hid = dy_ref[dp].reshape(256, D).astype(F32) + rms_back(hid, r, gain, d_b)
    dhid_ref[...] = d_hid
    datt[dp] = d_hid.astype(BF).reshape(2, 128, D)
    line.sent()
    line = LineGather(datt, d_send, d_recv)
    line.begin()
    scatter.sent()

    def back(block):
        do_ref[block_rows(block), :] = dot_t(datt[block].reshape(256, D), wout).astype(BF)

    def back_chip(offset):
        back(block_of(offset, False))
        back(block_of(offset, True))

    line.wait(6)
    back_chip(0)
    line.pass_on()
    line.second()
    line.wait(7, 8, 9, 10)
    back_chip(1)
    back_chip(3)
    line.third()
    line.wait(11, 12)
    back_chip(2)
    gout_ref[...] = t_dot(o_ref[...], datt[...].reshape(2048, D)).astype(BF).reshape(4, 4, 16, D)
    line.sent()


def mid(x, o, wout, wexp, wred, dy, gain):
    sh = jax.ShapeDtypeStruct
    return pl.pallas_call(
        mid_kernel,
        out_shape=(
            sh((256, D), F32),
            sh((256, D), F32),
            sh((2048, FF // 8), BF),
            sh((2048, 256), BF),
            sh((4, 4, RED_ROWS, D), BF),
            sh((4, 4, 64, EXP_COLS), BF),
            sh((4, 4, 16, D), BF),
            sh((8, D), F32),
            sh((FF // 8, D), BF),
        ),
        in_specs=[VMEM] * 7,
        out_specs=[VMEM] * 9,
        scratch_shapes=[
            pltpu.VMEM((D, D), BF),
            pltpu.VMEM((8, 2, 128, D), BF),
            pltpu.VMEM((8, 2, 128, D), BF),
            pltpu.VMEM((2048, EXP_COLS), BF),
            pltpu.VMEM((8, 128), F32),
        ]
        + line_scatter_scratch(128, D)[:5]
        + [pltpu.SemaphoreType.DMA((n,)) for n in (10, 10, 13, 13, 10, 10, 13, 13)],
        compiler_params=pltpu.CompilerParams(
            collective_id=3, has_side_effects=True, vmem_limit_bytes=60 * 2**20
        ),
        name="middle",
    )(x, o, wout, wexp, wred, dy, gain)


def in_three(values):
    high = values.astype(BF)
    rest = values - high.astype(F32)
    middle = rest.astype(BF)
    return high.astype(F32), middle.astype(F32), (rest - middle.astype(F32)).astype(BF).astype(F32)


def attend_back_block(
    i, q_ref, k_ref, v_ref, qx_ref, kx_ref, vx_ref, o_ref, lse_ref, do_ref,
    dq_ref, dk_ref, dv_ref, qs, dos, dqa,
):
    rows = block_rows(i)
    lane = lax.broadcasted_iota(jnp.int32, (BLOCK, HD), 1)
    for h in range(2):
        part = slice(h * BLOCK, (h + 1) * BLOCK)
        cols = slice(h * HD, (h + 1) * HD)
        qs[part, 0:HD] = q_ref[rows, cols]
        extra = qx_ref[rows, :].astype(F32)
        for k, term in enumerate(in_three(lse_ref[rows, h : h + 1])):
            extra = jnp.where(lane == 4 + k, -term, extra)
        qs[part, HD:] = extra.astype(BF)
        d = do_ref[rows, cols]
        dos[part, 0:HD] = d
        inner = jnp.sum(d.astype(F32) * o_ref[rows, cols].astype(F32), axis=1, keepdims=True)
        extra = jnp.zeros((BLOCK, HD), F32)
        for k, term in enumerate(in_three(inner)):
            extra = jnp.where(lane == k, -term, extra)
        dos[part, HD:] = extra.astype(BF)

    def step(kr, diagonal):
        kk = jnp.concatenate([k_ref[kr, :], kx_ref[kr, :]], axis=1)
        vv = jnp.concatenate([v_ref[kr, :], vx_ref[kr, :]], axis=1)
        p = jnp.exp2(dot_t(kk, qs[...]) * SCORE)
        if diagonal:
            index = lax.broadcasted_iota(jnp.int32, (BLOCK, 2 * BLOCK), 0)
            query = lax.broadcasted_iota(jnp.int32, (BLOCK, 2 * BLOCK), 1) & (BLOCK - 1)
            p = jnp.where(index <= query, p, 0.0)
        ds = (p * dot_t(vv, dos[...])).astype(BF)
        dv_ref[kr, :] += dot(p.astype(BF), dos[:, 0:HD])
        dk_ref[kr, :] += dot(ds, qs[:, 0:HD])
        dq = t_dot(ds, kk[:, 0:HD])
        if diagonal:
            dqa[...] = dq
        else:
            dqa[...] += dq

    step(rows, True)

    def wide(j, carry):
        step(wide_rows(j), False)
        return carry

    def narrow(j, carry):
        step(block_rows(j), False)
        return carry

    lax.fori_loop(0, i // 2, wide, 0)
    lax.fori_loop(i // 2 * 2, i, narrow, 0)
    for h in range(2):
        dq_ref[rows, h * HD : (h + 1) * HD] = dqa[h * BLOCK : (h + 1) * BLOCK, :] * HD**-0.5


def attention_back_kernel(
    q_ref, k_ref, v_ref, qx_ref, kx_ref, vx_ref, o_ref, lse_ref, do_ref,
    act_ref, wred_ref, hid_ref, pred_ref, pexp_ref, pout_ref,
    dq_ref, dk_ref, dv_ref, y_ref, gred_ref, gexp_ref, gout_ref,
    qs, dos, dqa, *rest,
):
    z, core, x, y = place()
    line_bufs, rest = rest[:7], rest[7:]
    planes = [
        PlaneScatter(part, *rest[5 * n : 5 * n + 5]) for n, part in enumerate((pred_ref, pexp_ref, pout_ref))
    ]
    scatter = LineScatter(*line_bufs)
    keep, give = line_bufs[0], line_bufs[1]
    meet(line_peers() + plane_peers())
    for plane in planes:
        plane.begin()
    for offset in (2, 1, 3, 0):
        chip = lax.rem(z + offset, 4) * 2
        give[offset] = (
            dot(act_ref[block_rows(chip + 1 - core), :], wred_ref[...]).astype(BF).reshape(2, 128, D)
        )
        scatter.give(offset)
        keep[offset] = dot(act_ref[block_rows(chip + core), :], wred_ref[...]).reshape(2, 128, D)
    scatter.far()
    scatter.near()
    dk_ref[...] = jnp.zeros_like(dk_ref)
    dv_ref[...] = jnp.zeros_like(dv_ref)

    def block(t, carry):
        attend_back_block(
            7 - t, q_ref, k_ref, v_ref, qx_ref, kx_ref, vx_ref, o_ref, lse_ref, do_ref,
            dq_ref, dk_ref, dv_ref, qs, dos, dqa,
        )

        @pl.when(t == 0)
        def _():
            scatter.last()

        @pl.when(t == 2)
        def _():
            for plane in planes:
                plane.pass_on()

        return carry

    lax.fori_loop(0, 8, block, 0)
    dk_ref[...] *= HD**-0.5
    first, second = scatter.result()
    y_ref[...] = (hid_ref[...] + jnp.concatenate([first, second], axis=0)).astype(BF)
    for plane, out in zip(planes, (gred_ref, gexp_ref, gout_ref)):
        plane.end(out)
        plane.sent()
    scatter.sent()


def attention_back(*args):
    sh = jax.ShapeDtypeStruct
    return pl.pallas_call(
        attention_back_kernel,
        out_shape=(
            sh((2048, 256), F32),
            sh((2048, 128), F32),
            sh((2048, 128), F32),
            sh((256, D), BF),
            sh((RED_ROWS, D), F32),
            sh((64, EXP_COLS), F32),
            sh((16, D), F32),
        ),
        in_specs=[VMEM] * 15,
        out_specs=[VMEM] * 7,
        scratch_shapes=[
            pltpu.VMEM((2 * BLOCK, 256), BF),
            pltpu.VMEM((2 * BLOCK, 256), BF),
            pltpu.VMEM((2 * BLOCK, HD), F32),
        ]
        + line_scatter_scratch(128, D)
        + plane_scatter_scratch(RED_ROWS, D)
        + plane_scatter_scratch(64, EXP_COLS)
        + plane_scatter_scratch(16, D),
        compiler_params=pltpu.CompilerParams(
            collective_id=4, has_side_effects=True, vmem_limit_bytes=60 * 2**20
        ),
        name="attention_back",
    )(*args)


def from_received(got, gin, gexp):
    col = 0
    for ref, start, width in (
        (gin, 0, 256),
        (gin, H * HD, 128),
        (gin, (H + KV) * HD, 128),
        (gexp, 0, 384),
        (gexp, FF, 384),
    ):
        for j in range(8):
            ref[:, start + j * width : start + (j + 1) * width] = got[j, :, col : col + width]
        col += width


def last_kernel(
    dq_ref, dk_ref, dv_ref, raw_ref, cos_ref, sin_ref, gain_ref, a_ref, win_ref, x_ref, dhid_ref, dmid_ref, gexp_ref,
    dx_ref, gin_out, gexp_out, dgain_ref,
    perm, dqkv, parts, gin, csend, cgot, gsum, gdp, gx, gy,
    keep, give, took, out_z, in_z, s_send, s_recv,
    got1, between, got2, p_send, p_recv, c_send, c_recv, g_send, g_recv,
):
    z, core, x, y = place()
    dp = lax.axis_index("dp")
    peers = dp_peers()
    meet(peers + plane_peers())
    scatter = LineScatter(keep, give, took, out_z, in_z, s_send, s_recv)
    plane = PlaneScatter(parts, got1, between, got2, p_send, p_recv)
    gsum[...] = jnp.zeros_like(gsum)

    def block(b):
        rows = block_rows(b)
        for part in range(3):
            cols = slice(part * HD, (part + 1) * HD)
            u = raw_ref[rows, cols]
            d = dq_ref[rows, cols] if part < 2 else dk_ref[rows, :]
            start = 2 * D + (HD if part == 2 else 0)
            gain = gain_ref[0:1, start : start + HD]
            d = d * cos_ref[rows, :] + pltpu.roll(d * sin_ref[rows, :], HD // 2, 1)
            r = normed_rows(u)
            row = 16 + part // 2
            gsum[row : row + 1, :] += jnp.sum(d * u * r, axis=0, keepdims=True)
            dqkv[rows, cols] = rms_back(u, r, gain, d).astype(BF)
        dqkv[rows, 384:512] = dv_ref[rows, :].astype(BF)
        return dot_t(dqkv[rows, :], win_ref[...].reshape(D, IN_COLS)).reshape(2, 128, D)

    for offset in (2, 1, 3, 0):
        chip = lax.rem(z + offset, 4) * 2
        give[offset] = block(chip + 1 - core).astype(BF)
        scatter.give(offset)
        keep[offset] = block(chip + core)
    scatter.far()
    scatter.near()
    parts[...] = t_dot(a_ref[...], dqkv[...]).astype(BF).reshape(4, 4, 64, IN_COLS)
    plane.begin()
    fill_order(perm)
    scatter.last()
    plane.pass_on()
    first, second = scatter.result()
    d_a = unorder(jnp.concatenate([first, second], axis=0), perm[...])
    values = x_ref[...].astype(F32)
    r = normed_rows(values)
    dx_ref[...] = dhid_ref[...] + rms_back(values, r, gain_ref[0:1, 0:D], d_a)
    d_in = jnp.sum(d_a * values * r, axis=0, keepdims=True)
    for k in range(8):
        gsum[k : k + 1, :] = d_in[:, k * 128 : (k + 1) * 128]
        gsum[8 + k : 9 + k, :] = dmid_ref[0:1, k * 128 : (k + 1) * 128]
    first_copies = [
        remote(gsum, gdp.at[k - 1], g_send.at[k - 1], g_recv.at[k - 1], peers[k - 1]) for k in range(1, 8)
    ]
    for copy in first_copies:
        copy.start()
    plane.end(gin)
    for d in range(8):
        csend[d, :, 0:IN_COLS] = gin[8 * d : 8 * d + 8, :]
        csend[d, :, IN_COLS:] = gexp_ref[8 * d : 8 * d + 8, :]
    cols = [
        remote(csend.at[lax.rem(dp + k, 8)], cgot.at[dp], c_send.at[k - 1], c_recv.at[k - 1], peers[k - 1])
        for k in range(1, 8)
    ]
    for copy in cols:
        copy.start()
    cgot[dp] = csend[dp]
    for copy in first_copies:
        copy.wait_recv()
    total = gsum[...]
    for k in range(7):
        total += gdp[k]
    gx[0] = total
    x_copies = [
        remote(gx.at[0], gx.at[k], g_send.at[6 + k], g_recv.at[6 + k], device(z, core, x + k, y)) for k in (1, 2, 3)
    ]
    for copy in x_copies:
        copy.start()
    for copy in x_copies:
        copy.wait_recv()
    gy[0] = gx[0] + gx[1] + gx[2] + gx[3]
    y_copies = [
        remote(gy.at[0], gy.at[k], g_send.at[9 + k], g_recv.at[9 + k], device(z, core, x, y + k)) for k in (1, 2, 3)
    ]
    for copy in y_copies:
        copy.start()
    for copy in cols:
        copy.wait_recv()
    from_received(cgot, gin_out, gexp_out)
    for copy in y_copies:
        copy.wait_recv()
    dgain_ref[...] = gy[0] + gy[1] + gy[2] + gy[3]
    for copy in first_copies + x_copies + y_copies + cols:
        copy.wait_send()
    scatter.sent()
    plane.sent()


def last(*args):
    sh = jax.ShapeDtypeStruct
    return pl.pallas_call(
        last_kernel,
        out_shape=(sh((256, D), F32), sh((8, 4096), F32), sh((8, 2 * FF), F32), sh((24, 128), F32)),
        in_specs=[VMEM] * 13,
        out_specs=[VMEM] * 4,
        scratch_shapes=[
            pltpu.VMEM((D, D), BF),
            pltpu.VMEM((2048, IN_COLS), BF),
            pltpu.VMEM((4, 4, 64, IN_COLS), BF),
            pltpu.VMEM((64, IN_COLS), F32),
            pltpu.VMEM((8, 8, IN_COLS + EXP_COLS), F32),
            pltpu.VMEM((8, 8, IN_COLS + EXP_COLS), F32),
            pltpu.VMEM((24, 128), F32),
            pltpu.VMEM((7, 24, 128), F32),
            pltpu.VMEM((4, 24, 128), F32),
            pltpu.VMEM((4, 24, 128), F32),
        ]
        + line_scatter_scratch(128, D)
        + plane_scatter_scratch(64, IN_COLS)
        + [pltpu.SemaphoreType.DMA((n,)) for n in (7, 7, 13, 13)],
        compiler_params=pltpu.CompilerParams(
            collective_id=5, has_side_effects=True, vmem_limit_bytes=60 * 2**20
        ),
        name="last",
    )(*args)


def body(
    tokens,
    cotangent,
    lengths,
    weight_input,
    weight_output,
    weight_expand,
    weight_reduce,
    gains,
    first_input,
    first_output,
    first_expand,
    first_reduce,
    first_gains,
    second_input,
    second_output,
    second_expand,
    second_reduce,
    second_gains,
):
    whole = tokens.shape[1] * lax.axis_size("dp")
    segment, cosine, sine = rope_full(lengths[0], whole)
    q_extra, k_extra, v_extra = extra_columns(segment)
    a, raw, q, k, v, win, wexp, gain, wout, wred = front(
        tokens[0],
        weight_input,
        weight_expand,
        padded_gains(gains),
        cosine,
        sine,
        weight_output,
        weight_reduce,
    )
    o, lse, wexp, dy = attention(q, k, v, q_extra, k_extra, v_extra, wexp, cotangent[0])
    hid, d_hid, act, d_o, part_red, part_exp, part_out, d_gain_mid, wred = mid(
        tokens[0], o, wout, wexp, wred, dy, gain
    )
    dq, dk, dv, block_out, sum_red, sum_exp, grad_output = attention_back(
        q, k, v, q_extra, k_extra, v_extra, o, lse, d_o, act, wred, hid, part_red, part_exp, part_out
    )
    input_grad, grad_input, grad_expand, grad_gains = last(
        dq, dk, dv, raw, cosine, sine, gain, a, win, tokens[0], d_hid, d_gain_mid, sum_exp
    )
    block_out = block_out[None]
    input_grad = input_grad[None]
    grad_reduce = sum_red[: weight_reduce.shape[0]]
    own = gains.shape[0]
    index = lax.axis_index("dp") * lax.axis_size("shard") + lax.axis_index("shard")
    grad_gains = lax.dynamic_slice_in_dim(grad_gains.reshape(-1), index * own, own)
    new_input, mean_input, square_input = adam_step(
        weight_input, grad_input, first_input, second_input, matrix_rate, matrix_decay
    )
    new_output, mean_output, square_output = adam_step(
        weight_output, grad_output, first_output, second_output, matrix_rate, matrix_decay
    )
    new_expand, mean_expand, square_expand = adam_step(
        weight_expand, grad_expand, first_expand, second_expand, matrix_rate, matrix_decay
    )
    new_reduce, mean_reduce, square_reduce = adam_step(
        weight_reduce, grad_reduce, first_reduce, second_reduce, matrix_rate, matrix_decay
    )
    new_gains, mean_gains, square_gains = adam_step(
        gains, grad_gains, first_gains, second_gains, gain_rate, 0.0
    )
    return (
        block_out,
        input_grad,
        new_input,
        new_output,
        new_expand,
        new_reduce,
        new_gains,
        mean_input,
        mean_output,
        mean_expand,
        mean_reduce,
        mean_gains,
        square_input,
        square_output,
        square_expand,
        square_reduce,
        square_gains,
    )


def solution(mesh):
    placed = (
        P("shard", "dp", None),
        P("shard", "dp", None),
        P("shard", None),
        P(("dp", "shard"), None),
        P(("dp", "shard"), None),
        P(("dp", "shard"), None),
        P(("dp", "shard"), None),
        P(("dp", "shard")),
        P(("dp", "shard"), None),
        P(("dp", "shard"), None),
        P(("dp", "shard"), None),
        P(("dp", "shard"), None),
        P(("dp", "shard")),
        P(("dp", "shard"), None),
        P(("dp", "shard"), None),
        P(("dp", "shard"), None),
        P(("dp", "shard"), None),
        P(("dp", "shard")),
    )
    return jax.shard_map(
        body,
        mesh=mesh,
        in_specs=placed,
        out_specs=(
            P("shard", "dp", None),
            P("shard", "dp", None),
            P(("dp", "shard"), None),
            P(("dp", "shard"), None),
            P(("dp", "shard"), None),
            P(("dp", "shard"), None),
            P(("dp", "shard")),
            P(("dp", "shard"), None),
            P(("dp", "shard"), None),
            P(("dp", "shard"), None),
            P(("dp", "shard"), None),
            P(("dp", "shard")),
            P(("dp", "shard"), None),
            P(("dp", "shard"), None),
            P(("dp", "shard"), None),
            P(("dp", "shard"), None),
            P(("dp", "shard")),
        ),
        check_vma=False,
    )
```

time: 843 us -> 300 us (0.36)
  waiting for transfers between devices: 325 us -> 0 us
  Pallas kernels: 0 us -> 277 us
  blocking collectives: 199 us -> 0 us
  matrix products: 169 us -> 0 us
  other arithmetic: 85.3 us -> 16.1 us
  local copies, waits for them, and re-layouts: 29.2 us -> 4.02 us
  between operations: 17.7 us -> 1.16 us
  starting transfers between devices: 8.58 us -> 0 us
    pallas_call x0 -> x5, Pallas kernels: none -> 277 us  [the longest x1 97.2 us: mid(): pl.pallas_call(mid_kernel, out_shape=(sh((256, D), F32), sh((256, D), F32...]
    dot_general x26 -> x0, matrix products: 169 us -> none  [the longest x10 81.1 us: dot_t(): lax.dot_general(a, b, (((1,), (1,)), ((), ())), preferred_element_type=jn...]
    reduce_scatter x5 -> x0, waiting for transfers between devices: 132 us -> none  [the longest x4 81.9 us: scatter_tokens(): lax.psum_scatter(partial.astype(jnp.bfloat16), 'dp', scatter_dimension=0,...]
    unnamed x3 -> x0, blocking collectives: 130 us -> none
    unnamed x15 -> x0, waiting for transfers between devices: 95 us -> none
    all_gather x6 -> x0, waiting for transfers between devices: 88.8 us -> none  [the longest x4 73.6 us: gather_tokens(): return lax.all_gather(block, 'dp', axis=0, tiled=True)]
    all_gather x2 -> x0, blocking collectives: 49 us -> none  [gather_rows(): lax.all_gather(weight.astype(jnp.bfloat16), 'shard', axis=0, tiled=True)]
    convert_element_type x10 -> x3, other arithmetic: 30.2 us -> 2.29 us  [the longest x1 1.15 us: extra_columns(): jnp.where(lane < 4, same.astype(F32), jnp.where(lane < 7, 1.0, 0.0))]
  transfers between devices with their start and end apart: 15 -> 0, of which waited for: 11 -> 0; matrix products, arithmetic and copies ran while one was open for 21% -> 0% of each run, Pallas kernels for 0% -> 0%
where the time goes in v2:
time: 300 us; the launch traced here: 299 us
  Pallas kernels  277 us (92%)
  other arithmetic  16.1 us (5%)
  local copies, waits for them, and re-layouts  4.02 us (1%)
    pallas_call x1, Pallas kernels, mid(): pl.pallas_call(mid_kernel, out_shape=(sh((256, D), F32), sh((256, D), F32...  97.2 us
    pallas_call x1, Pallas kernels, front(): pl.pallas_call(front_kernel, out_shape=(sh((2048, D), BF), sh((2048, 384)...  59.7 us
    pallas_call x1, Pallas kernels, last(): pl.pallas_call(last_kernel, out_shape=(sh((256, D), F32), sh((8, 4096), F...  51.8 us
    pallas_call x1, Pallas kernels, attention_back(): pl.pallas_call(attention_back_kernel, out_shape=(sh((2048, 256), F32), sh...  39.4 us
    pallas_call x1, Pallas kernels, attention(): pl.pallas_call(attention_kernel, out_shape=(sh((2048, 256), BF), sh((2048...  29.3 us
    sub x5, other arithmetic, adam_step(): return (weight - rate * (direction + decay * weight), first_new, second_new)  6.47 us

profile of v2, /device:TPU:0, one launch (start us, length us, event | category | flops | bytes accessed | tf_op | source)
XLA Modules:
  0.0 298.6 jit_solution(1300882743080790325)
XLA Ops:
  0.7 0.7 pad.4
  1.3 0.6 broadcast_in_dim.58.gains_ref
  1.9 0.8 reduce-window.4
  2.8 0.7 fusion.8
  3.4 0.1 convert_reduce_fusion
  3.5 0.1 select_reduce_fusion
  3.6 3.7 %fusion.2 = (f32[2048,64]{1,0:T(8,128)S(1)}, f32[2048,64]{1,0:T(8,128)S(1)}, f32[2048,64]{1,0:T(8,128)S(1)}) fusion(f32[64]{0:T(128)S(1)} %multiply_power_fusion, f32[2048]{0:T(1024)S(1)} %subtract_convert_fusion), kind=kLoop, calls=%fused_computation.9 | loop fusion | flops 262144 | bytes 1581312 | tf_op jit(solution)/shard_map/neg | solution.py:573
  7.3 1.9 pad_maximum_fusion
  9.3 59.7 %front.1 = (bf16[2048,1024]{1,0:T(8,128)(2,1)}, f32[2048,384]{1,0:T(8,128)}, bf16[2048,256]{1,0:T(8,128)(2,1)}, bf16[2048,128]{1,0:T(8,128)(2,1)}, bf16[2048,128...) custom-call(bf16[256,1024]{1,0:T(8,128)(2,1)} %bitcast.13, ...), custom_call_target="tpu_custom_call" | custom-call | tf_op jit(solution)/shard_map/front/pallas_call | solution.py:536
  69.0 1.1 select_convert_fusion.1.qx_ref
  70.2 1.2 select_convert_fusion.kx_ref
  71.3 0.9 broadcast_in_dim.64.vx_ref
  72.2 29.3 %attention.1 = (bf16[2048,256]{1,0:T(8,128)(2,1)}, f32[2048,128]{1,0:T(8,128)}, bf16[4,4,64,768]{3,2,1,0:T(8,128)(2,1)}, bf16[8,2,128,1024]{3,2,1,0:T(8,128)(2,1)}) custom-call(bf16[2048,256]{1,0:T(8,128)(2,1)} %get-tuple-element.51.q_ref, bf16[2048,128]{1,0:T(8,128)(2,1)} %get-tuple-element.52.k_ref, bf16[2048,128]{1,0:T(8,128)(2,1)} %get-tuple-element.53.v_ref, ...), custom_call_target="tpu_custom_call" | custom-call | tf_op jit(solution)/shard_map/attention/pallas_call | solution.py:685
  101.5 97.2 %middle.1 = (f32[256,1024]{1,0:T(8,128)}, f32[256,1024]{1,0:T(8,128)}, bf16[2048,384]{1,0:T(8,128)(2,1)}, bf16[2048,256]{1,0:T(8,128)(2,1)}, bf16[4,4,32,1024]{3...) custom-call(bf16[256,1024]{1,0:T(8,128)(2,1)} %bitcast.14, ...), custom_call_target="tpu_custom_call" | custom-call | tf_op jit(solution)/shard_map/middle/pallas_call | solution.py:824
  198.6 39.4 %attention_back.1 = (f32[2048,256]{1,0:T(8,128)}, f32[2048,128]{1,0:T(8,128)}, f32[2048,128]{1,0:T(8,128)}, bf16[256,1024]{1,0:T(8,128)(2,1)}, f32[32,1024]{1,0:...) custom-call(bf16[2048,256]{1,0:T(8,128)(2,1)} %get-tuple-element.51.q_ref, bf16[2048,128]{1,0:T(8,128)(2,1)} %get-tuple-element.52.k_ref, ...), custom_call_target="tpu_custom_call" | custom-call | tf_op jit(solution)/shard_map/attention_back/pallas_call | solution.py:974
  238.1 0.0 copy-start.2
  238.1 0.0 copy-start.8
  238.1 0.0 copy-start.9
  238.1 0.0 copy-start.5
  238.1 0.0 copy-start.13
  238.1 0.0 copy-start.14
  238.1 0.0 copy-start.15
  238.2 0.0 copy-start.1
  238.2 0.0 copy-start.6
  238.2 0.0 copy-start.7
  238.2 51.8 %last.1 = (f32[256,1024]{1,0:T(8,128)}, f32[8,4096]{1,0:T(8,128)}, f32[8,6144]{1,0:T(8,128)}, f32[24,128]{1,0:T(8,128)}) custom-call(f32[2048,256]{1,0:T(8,128)} %get-tuple-element.70.dq_ref, f32[2048,128]{1,0:T(8,128)} %get-tuple-element.71.dk_ref, f32[2048,128]{1,0:T(8,128)} %get-tuple-element.72.dv_ref, f32[2048,384]{1,0:T(8,128)} %get-tuple-element.73.raw_ref, ...), custom_call_target="tpu_custom_call" | custom-call | tf_op jit(solution)/shard_map/last/pallas_call | solution.py:1118
  290.0 0.0 copy-start.4
  290.0 0.0 copy-start.10
  290.0 0.0 copy-start.11
  290.0 0.0 copy-start.12
  290.0 0.0 copy-start.16
  290.0 0.0 copy-start.17
  290.0 0.0 copy-start.18
  290.0 0.0 copy-start.3
  290.1 0.0 copy-done.2
  290.1 0.0 copy-done.8
  290.1 0.0 copy-done.9
  290.1 0.0 copy-start
  290.1 1.9 multiply_subtract_fusion.1
  292.0 0.0 copy-done.5
  292.0 0.0 copy-done.13
  292.0 0.0 copy-done.14
  292.0 0.0 copy-done.15
  292.0 0.7 multiply_subtract_fusion.3
  292.7 0.0 copy-done.1
  292.7 0.0 copy-done.6
  292.7 0.0 copy-done.7
  292.7 1.8 multiply_subtract_fusion
  294.5 0.0 copy-done.4
  294.5 0.0 copy-done.10
  294.5 0.0 copy-done.11
  294.5 0.0 copy-done.12
  294.5 0.7 multiply_subtract_fusion.2
  295.3 0.0 copy-done.16
  295.3 0.0 copy-done.17
  295.3 0.0 copy-done.18
  295.3 1.3 multiply_subtract_fusion.4
  296.6 0.0 copy-done.3
  296.6 0.8 copy.37
  297.4 0.0 copy-done
  297.4 1.0 copy.38
  (5 shorter events, 0.0 us)
Async XLA Ops:
  238.1 52.0 %copy-start.2 = (f32[8,4096]{1,0:T(8,128)S(1)}, f32[8,4096]{1,0:T(8,128)}, u32[]{:S(2)}) copy-start(f32[8,4096]{1,0:T(8,128)} %w_in_ref.1) | copy-start | bytes 393220
  238.1 52.0 %copy-start.8 = (f32[8,4096]{1,0:T(8,128)S(1)}, f32[8,4096]{1,0:T(8,128)}, u32[]{:S(2)}) copy-start(f32[8,4096]{1,0:T(8,128)} %param.26) | copy-start | bytes 393220
  238.1 52.0 %copy-start.9 = (f32[8,4096]{1,0:T(8,128)S(1)}, f32[8,4096]{1,0:T(8,128)}, u32[]{:S(2)}) copy-start(f32[8,4096]{1,0:T(8,128)} %param.31) | copy-start | bytes 393220
  238.1 53.9 %copy-start.5 = (f32[16,1024]{1,0:T(8,128)S(1)}, f32[16,1024]{1,0:T(8,128)}, u32[]{:S(2)}) copy-start(f32[16,1024]{1,0:T(8,128)} %w_out_ref.1) | copy-start | bytes 196612
  238.1 53.9 %copy-start.13 = (f32[16,1024]{1,0:T(8,128)S(1)}, f32[16,1024]{1,0:T(8,128)}, u32[]{:S(2)}) copy-start(f32[16,1024]{1,0:T(8,128)} %param.27) | copy-start | bytes 196612
  238.1 53.9 %copy-start.14 = (f32[16,1024]{1,0:T(8,128)S(1)}, f32[16,1024]{1,0:T(8,128)}, u32[]{:S(2)}) copy-start(f32[16,1024]{1,0:T(8,128)} %param.32) | copy-start | bytes 196612
  238.1 53.9 %copy-start.15 = (f32[16,1024]{1,0:T(8,128)S(1)}, f32[16,1024]{1,0:T(8,128)}, u32[]{:S(2)}) copy-start(f32[16,1024]{1,0:T(8,128)} %get-tuple-element.81) | copy-start | bytes 196612
  238.2 54.5 %copy-start.1 = (f32[8,6144]{1,0:T(8,128)S(1)}, f32[8,6144]{1,0:T(8,128)}, u32[]{:S(2)}) copy-start(f32[8,6144]{1,0:T(8,128)} %w_exp_ref.1) | copy-start | bytes 589828
  238.2 54.5 %copy-start.6 = (f32[8,6144]{1,0:T(8,128)S(1)}, f32[8,6144]{1,0:T(8,128)}, u32[]{:S(2)}) copy-start(f32[8,6144]{1,0:T(8,128)} %param.28) | copy-start | bytes 589828
  238.2 54.5 %copy-start.7 = (f32[8,6144]{1,0:T(8,128)S(1)}, f32[8,6144]{1,0:T(8,128)}, u32[]{:S(2)}) copy-start(f32[8,6144]{1,0:T(8,128)} %param.33) | copy-start | bytes 589828
  290.0 4.6 %copy-start.4 = (f32[24,1024]{1,0:T(8,128)S(1)}, f32[24,1024]{1,0:T(8,128)}, u32[]{:S(2)}) copy-start(f32[24,1024]{1,0:T(8,128)} %w_red_ref.1) | copy-start | bytes 294916
  290.0 4.6 %copy-start.10 = (f32[24,1024]{1,0:T(8,128)S(1)}, f32[24,1024]{1,0:T(8,128)}, u32[]{:S(2)}) copy-start(f32[24,1024]{1,0:T(8,128)} %param.29) | copy-start | bytes 294916
  290.0 4.6 %copy-start.11 = (f32[24,1024]{1,0:T(8,128)S(1)}, f32[24,1024]{1,0:T(8,128)}, u32[]{:S(2)}) copy-start(f32[24,1024]{1,0:T(8,128)} %param.34) | copy-start | bytes 294916
  290.0 4.5 %copy-start.12 = (f32[32,1024]{1,0:T(8,128)S(1)}, f32[32,1024]{1,0:T(8,128)}, u32[]{:S(2)}) copy-start(f32[32,1024]{1,0:T(8,128)} %get-tuple-element.83) | copy-start | bytes 393220
  290.0 5.3 %copy-start.16 = (f32[18]{0:T(128)S(1)}, f32[18]{0:T(128)}, u32[]{:S(2)}) copy-start(f32[18]{0:T(128)} %param.25) | copy-start | bytes 220
  290.0 5.3 %copy-start.17 = (f32[18]{0:T(128)S(1)}, f32[18]{0:T(128)}, u32[]{:S(2)}) copy-start(f32[18]{0:T(128)} %param.30) | copy-start | bytes 220
  290.0 5.3 %copy-start.18 = (f32[18]{0:T(128)S(1)}, f32[18]{0:T(128)}, u32[]{:S(2)}) copy-start(f32[18]{0:T(128)} %param.35) | copy-start | bytes 220
  290.0 6.6 %copy-start.3 = (bf16[256,1024]{1,0:T(8,128)(2,1)S(1)}, bf16[256,1024]{1,0:T(8,128)(2,1)}, u32[]{:S(2)}) copy-start(bf16[256,1024]{1,0:T(8,128)(2,1)} %get-tuple-element.69) | copy-start | bytes 1572868
  290.1 7.3 %copy-start = (f32[256,1024]{1,0:T(8,128)S(1)}, f32[256,1024]{1,0:T(8,128)}, u32[]{:S(2)}) copy-start(f32[256,1024]{1,0:T(8,128)} %get-tuple-element.79) | copy-start | bytes 3145732
